TPU v7x, 32 devices: a whole 2x2x4 slice. The times are simulated.
32 devices in a mesh: groups: 2 (over y), tile: 4 (over z), segment: 2 (over core), mp: 2 (over x).
Axes of the slice: x: 2, y: 2, z: 4, core: 2. Of those that a mesh axis runs over, the one named last changes fastest.
Arguments:
- spectra: bfloat16 [2, 64, 48, 224], P(None, ('groups', 'tile')), parts along dimension 1, may hold values from -6 to 6
- valid: int32 [2, 64], P(None, 'groups'), parts along dimension 1, may hold values from 1 to 48, as said below
- project: bfloat16 [224, 16], replicated, may hold values from -0.375 to 0.375
- enc_in: bfloat16 [768, 3072], P(None, 'mp'), may hold values from -0.21875 to 0.21875
- enc_out: bfloat16 [3072, 768], P('mp'), may hold values from -0.109375 to 0.109375
- tok_embed: bfloat16 [48, 2048], replicated, may hold values from -0.875 to 0.875
- band_embed: bfloat16 [16, 2048], P('tile'), may hold values from -3 to 3
- dec_in: bfloat16 [2048, 8192], P('tile', 'mp'), may hold values from -0.125 to 0.125
- dec_out: bfloat16 [8192, 2048], P('mp', 'tile'), may hold values from -0.0625 to 0.0625
- head: bfloat16 [2048, 672], P('tile', 'mp'), may hold values from -0.125 to 0.125
Outputs:
- grad_project: float32 [448, 16], P(('groups', 'tile', 'segment')), parts along dimension 0
- grad_enc_in: float32 [1536, 3072], P(('groups', 'tile', 'segment'), 'mp'), parts along dimension 0
- grad_enc_out: float32 [6144, 768], P(('groups', 'mp'), ('tile', 'segment')), parts along dimension 0
There are 2 independent parts, one for each index of `groups`. A program takes and returns all parts, laid end to end along the dimension named above; an argument that names none is the same for every part. Nothing has to cross between parts.
Inputs may be any that keep to these rules, and one draw needn't show every extreme that they name: Pixels of patch n in micro-batch m with index below valid[m, n] count in the loss.
All inputs are finite; a program needn't handle non-finite values.
Results may differ from a plain program's by a relative error of at most 0.018.
Values may be sent and summed in bfloat16 or wider, within the bound.
A program may use at most 128 MiB of HBM per device.

v0:
```python
import jax
import jax.numpy as jnp
from jax import lax
from jax.sharding import PartitionSpec as P


def from_partner(array, axis, stride):
    return lax.ppermute(array, axis, [(i, i ^ 1 << stride) for i in range(lax.axis_size(axis))])


def rms_norm(values):
    return values * lax.rsqrt(jnp.mean(values * values, axis=-1, keepdims=True) + 1e-05)


def rms_back(values, gradient):
    scaling = lax.rsqrt(jnp.mean(values * values, axis=-1, keepdims=True) + 1e-05)
    normed = values * scaling
    return scaling * (gradient - normed * jnp.mean(gradient * normed, axis=-1, keepdims=True))


def gelu_tanh(values):
    return jax.nn.gelu(values, approximate=True)


def gelu_back(pre_values, gradient):
    return jax.vjp(gelu_tanh, pre_values)[1](gradient)[0]


def dot_plain(operand, factor):
    return jnp.dot(operand, factor, preferred_element_type=jnp.float32)


def dot_rows(operand, factor):
    return lax.dot_general(
        operand, factor, (((1,), (1,)), ((), ())), preferred_element_type=jnp.float32
    )


def dot_cols(operand, factor):
    return lax.dot_general(
        operand, factor, (((0,), (0,)), ((), ())), preferred_element_type=jnp.float32
    )


def on_segment(active, function):

    def silent():
        return jax.tree.map(jnp.zeros_like, function())

    return lax.cond(active, function, silent)


def body(spectra, valid, project, enc_in, enc_out, tok_embed, band_embed, dec_in, dec_out, head):
    first_segment = lax.axis_index("segment") == 0
    later_segment = jnp.logical_not(first_segment)
    mp_rank = lax.axis_index("mp")
    mp_count = lax.axis_size("mp")
    tile_count = lax.axis_size("tile")
    local_patches = spectra.shape[1]
    pixel_width = spectra.shape[2]
    band_total = spectra.shape[3]
    code_count = project.shape[1]
    group_width = band_total // code_count
    pixel_share = pixel_width // mp_count
    local_bands = band_embed.shape[0]
    patch_total = valid.shape[1]
    total_valid = jnp.sum(valid.astype(jnp.float32))
    loss_scale = 2.0 * valid.shape[0] * patch_total / total_valid
    w_in, w_out, w_head = (
        lax.all_gather(dec_in, "tile", axis=0, tiled=True),
        lax.all_gather(dec_out, "tile", axis=1, tiled=True),
        lax.all_gather(head, "tile", axis=0, tiled=True),
    )

    def student_local(microbatch):
        pixels = spectra[microbatch].reshape(-1, band_total)
        band_codes = dot_plain(pixels, project).astype(jnp.bfloat16)
        features = (
            band_codes.reshape(local_patches, pixel_width, code_count)
            .transpose(0, 2, 1)
            .reshape(local_patches, -1)
        )
        normed = rms_norm(features.astype(jnp.float32)).astype(jnp.bfloat16)
        pre_act = dot_plain(normed, enc_in)
        act_out = gelu_tanh(pre_act).astype(jnp.bfloat16)
        return (features, normed, pre_act, act_out, dot_plain(act_out, enc_out))

    def student_forward(microbatch):
        features, normed, pre_act, act_out, partial_value = on_segment(
            first_segment, lambda: student_local(microbatch)
        )
        summed = lax.psum(partial_value.astype(jnp.bfloat16), "mp").astype(jnp.float32)
        encoded = (features.astype(jnp.float32) + summed).astype(jnp.bfloat16)
        own_pixels = lax.dynamic_slice_in_dim(
            spectra[microbatch], mp_rank * pixel_share, pixel_share, 1
        )
        target = (
            own_pixels.reshape(local_patches, pixel_share, code_count, group_width)
            .transpose(0, 2, 1, 3)
            .reshape(local_patches, code_count, -1)
        )
        payload = jnp.concatenate(
            [encoded.reshape(local_patches, code_count, pixel_width), target], axis=2
        )
        return (payload, (features, normed, pre_act, act_out))

    def hand_over(payload):
        relaid = lax.all_to_all(payload, "tile", split_axis=1, concat_axis=0, tiled=True)
        return from_partner(relaid, "segment", 0)

    def teacher(received, microbatch):
        row_count = received.shape[0] * received.shape[1]
        band_tok = received[:, :, :pixel_width].reshape(row_count, pixel_width)
        target = received[:, :, pixel_width:].reshape(row_count, -1)
        band_rows = jnp.tile(band_embed.astype(jnp.float32), (received.shape[0], 1))
        patch_valid = jnp.repeat(valid[microbatch], local_bands)
        pixel_index = mp_rank * pixel_share + jnp.arange(pixel_share, dtype=jnp.int32)
        valid_mask = (pixel_index[None, :] < patch_valid[:, None]).astype(jnp.float32)
        valid_mask = jnp.repeat(valid_mask, group_width, axis=1)

        def forward_part():
            embedded = (dot_plain(band_tok, tok_embed) + band_rows).astype(jnp.bfloat16)
            start_norm = rms_norm(embedded.astype(jnp.float32)).astype(jnp.bfloat16)
            hid_pre = dot_plain(start_norm, w_in)
            hid_act = gelu_tanh(hid_pre).astype(jnp.bfloat16)
            return (embedded, hid_pre, dot_plain(hid_act, w_out))

        embedded, hid_pre, partial_value = on_segment(later_segment, forward_part)
        summed = lax.psum(partial_value.astype(jnp.bfloat16), "mp").astype(jnp.float32)
        decoded = (embedded.astype(jnp.float32) + summed).astype(jnp.bfloat16)

        def head_part():
            rebuilt = dot_plain(decoded, w_head)
            grad_rebuilt = (
                loss_scale * valid_mask * (rebuilt - target.astype(jnp.float32))
            ).astype(jnp.bfloat16)
            return dot_rows(grad_rebuilt, w_head)

        grad_decoded = lax.psum(
            on_segment(later_segment, head_part).astype(jnp.bfloat16), "mp"
        ).astype(jnp.float32)

        def hidden_part():
            grad_act = dot_rows(grad_decoded.astype(jnp.bfloat16), w_out)
            grad_hid = gelu_back(hid_pre, grad_act).astype(jnp.bfloat16)
            return dot_rows(grad_hid, w_in)

        grad_norm = lax.psum(
            on_segment(later_segment, hidden_part).astype(jnp.bfloat16), "mp"
        ).astype(jnp.float32)

        def input_part():
            grad_start = (grad_decoded + rms_back(embedded.astype(jnp.float32), grad_norm)).astype(
                jnp.bfloat16
            )
            return dot_rows(grad_start, tok_embed).astype(jnp.bfloat16)

        grad_tok = on_segment(later_segment, input_part)
        arranged = (
            grad_tok.reshape(tile_count, local_patches, local_bands, pixel_width)
            .transpose(1, 0, 2, 3)
            .reshape(local_patches, code_count, pixel_width)
        )
        padding = jnp.zeros(
            (local_patches, code_count, received.shape[2] - pixel_width), jnp.bfloat16
        )
        return jnp.concatenate([arranged, padding], axis=2)

    def student_backward(received, microbatch, saved_state):
        grad_encoded = (
            received[:, :, :pixel_width]
            .reshape(tile_count, local_patches, local_bands, pixel_width)
            .transpose(1, 0, 2, 3)
            .reshape(local_patches, -1)
        )

        def local_grads():
            features, normed, pre_act, act_out = saved_state
            grad_out = dot_cols(act_out, grad_encoded)
            grad_act = gelu_back(pre_act, dot_rows(grad_encoded, enc_out)).astype(jnp.bfloat16)
            grad_in = dot_cols(normed, grad_act)
            return (features, grad_out, grad_in, dot_rows(grad_act, enc_in))

        features, grad_out, grad_in, partial_value = on_segment(first_segment, local_grads)
        grad_normed = lax.psum(partial_value.astype(jnp.bfloat16), "mp").astype(jnp.float32)

        def project_part():
            grad_feat = (
                grad_encoded.astype(jnp.float32)
                + rms_back(features.astype(jnp.float32), grad_normed)
            ).astype(jnp.bfloat16)
            grad_codes = (
                grad_feat.reshape(local_patches, code_count, pixel_width)
                .transpose(0, 2, 1)
                .reshape(-1, code_count)
            )
            return dot_cols(spectra[microbatch].reshape(-1, band_total), grad_codes)

        grad_proj = on_segment(first_segment, project_part)
        return (grad_proj, grad_in, grad_out)

    payload_first, saved_first = student_forward(0)
    received = hand_over(payload_first)
    payload_second, saved_second = student_forward(1)
    returned = teacher(received, 0)
    received = hand_over(jnp.where(first_segment, payload_second, returned))
    grads_first = student_backward(received, 0, saved_first)
    returned = teacher(received, 1)
    received = hand_over(returned)
    grads_second = student_backward(received, 1, saved_second)
    proj_total = grads_first[0] + grads_second[0]
    in_total = grads_first[1] + grads_second[1]
    out_total = grads_first[2] + grads_second[2]
    grad_proj, grad_in, grad_out = (
        lax.psum_scatter(
            proj_total.astype(jnp.bfloat16), ("tile", "segment"), scatter_dimension=0, tiled=True
        ).astype(jnp.float32),
        lax.psum_scatter(
            in_total.astype(jnp.bfloat16), ("tile", "segment"), scatter_dimension=0, tiled=True
        ).astype(jnp.float32),
        lax.psum_scatter(
            out_total.astype(jnp.bfloat16), ("tile", "segment"), scatter_dimension=1, tiled=True
        ).astype(jnp.float32),
    )
    return (grad_proj, grad_in, grad_out)


def solution(mesh):
    placed = (
        P(None, ("groups", "tile"), None, None),
        P(None, "groups"),
        P(),
        P(None, "mp"),
        P("mp", None),
        P(),
        P("tile", None),
        P("tile", "mp"),
        P("mp", "tile"),
        P("tile", "mp"),
    )
    return jax.shard_map(
        body,
        mesh=mesh,
        in_specs=placed,
        out_specs=(
            P(("groups", "tile", "segment"), None),
            P(("groups", "tile", "segment"), "mp"),
            P(("groups", "mp"), ("tile", "segment")),
        ),
        check_vma=False,
    )
```

profile of v0, /device:TPU:0, one launch (start us, length us, event | category | flops | bytes accessed | tf_op | source)
XLA Modules:
  0.0 1037.6 jit_solution(1318154049719847836)
XLA Ops:
  9.6 5.6 conditional.14
  15.2 5.6 conditional.15
  20.8 9.7 all-reduce.4
  35.2 17.8 %all_to_all.54 = bf16[8,16,384]{2,0,1:T(8,128)(2,1)S(1)} all-to-all(bf16[8,16,384]{2,0,1:T(8,128)(2,1)S(1)} %copy.82), channel_id=1, replica_groups=mesh['groups'=2,'tile'=4,'segment'=2,'mp'=2] {'tile'}, dimensions={1} | all-to-all | bytes 196608 | tf_op jit(solution)/shard_map/all_to_all | solution.py:108
  55.8 245.3 %all-gather.4.cloned.1.call-done = bf16[2048,4096]{1,0:T(8,128)(2,1)} async-done(((bf16[512,4096]{1,0:T(8,128)(2,1)}), bf16[2048,4096]{1,0:T(8,128)(2,1)}) %all-gather.4.cloned.1.call-update) | async-done | bytes 16777232 | tf_op jit(solution)/shard_map/all_gather | solution.py:70
  301.1 286.5 %all-gather.6.cloned.1.call-done = bf16[4096,2048]{1,0:T(8,128)(2,1)} async-done(((bf16[4096,512]{1,0:T(8,128)(2,1)}), bf16[4096,2048]{1,0:T(8,128)(2,1)}) %all-gather.6.cloned.1.call-update) | async-done | bytes 16777232 | tf_op jit(solution)/shard_map/all_gather | solution.py:71
  602.4 32.3 %all-reduce.12.cloned.1.call-done = bf16[128,2048]{1,0:T(8,128)(2,1)} async-done(((bf16[128,2048]{1,0:T(8,128)(2,1)}), bf16[128,2048]{1,0:T(8,128)(2,1)}) %all-reduce.12.cloned.1.call-update) | async-done | bytes 524304 | tf_op jit(solution)/shard_map/psum | solution.py:129
  636.7 36.7 %all-gather.8.cloned.1.call-done = bf16[2048,336]{1,0:T(8,128)(2,1)} async-done(((bf16[512,336]{1,0:T(8,128)(2,1)}), bf16[2048,336]{1,0:T(8,128)(2,1)}) %all-gather.8.cloned.1.call-update) | async-done | bytes 1376272 | tf_op jit(solution)/shard_map/all_gather | solution.py:72
  674.5 34.3 %all-reduce.14.cloned.1.call-done = bf16[128,2048]{1,0:T(8,128)(2,1)} async-done(((bf16[128,2048]{1,0:T(8,128)(2,1)}), bf16[128,2048]{1,0:T(8,128)(2,1)}) %all-reduce.14.cloned.1.call-update) | async-done | bytes 524304 | tf_op jit(solution)/shard_map/psum | solution.py:139
  718.0 37.6 %all-reduce.16.cloned.1.call-done = bf16[128,2048]{1,0:T(8,128)(2,1)} async-done(((bf16[128,2048]{1,0:T(8,128)(2,1)}), bf16[128,2048]{1,0:T(8,128)(2,1)}) %all-reduce.16.cloned.1.call-update) | async-done | bytes 524304 | tf_op jit(solution)/shard_map/psum | solution.py:148
  757.9 10.2 all_to_all.55
  768.2 3.0 collective-permute-start.1
  776.4 42.8 %all-reduce.18.cloned.1.call-done = bf16[128,2048]{1,0:T(8,128)(2,1)} async-done(((bf16[128,2048]{1,0:T(8,128)(2,1)}), bf16[128,2048]{1,0:T(8,128)(2,1)}) %all-reduce.18.cloned.1.call-update) | async-done | bytes 524304 | tf_op jit(solution)/shard_map/psum | solution.py:129
  822.1 34.3 %all-reduce.20.cloned.1.call-done = bf16[128,2048]{1,0:T(8,128)(2,1)} async-done(((bf16[128,2048]{1,0:T(8,128)(2,1)}), bf16[128,2048]{1,0:T(8,128)(2,1)}) %all-reduce.20.cloned.1.call-update) | async-done | bytes 524304 | tf_op jit(solution)/shard_map/psum | solution.py:139
  858.5 44.8 %all-reduce.22.cloned.1.call-done = bf16[128,2048]{1,0:T(8,128)(2,1)} async-done(((bf16[128,2048]{1,0:T(8,128)(2,1)}), bf16[128,2048]{1,0:T(8,128)(2,1)}) %all-reduce.22.cloned.1.call-update) | async-done | bytes 524304 | tf_op jit(solution)/shard_map/psum | solution.py:148
  903.4 10.2 all_to_all.56
  913.7 3.0 collective-permute-start.2
  916.8 17.0 %conditional.20 = (bf16[8,768]{1,0:T(8,128)(2,1)}, bf16[8,768]{1,0:T(8,128)(2,1)S(1)}, f32[768,1536]{1,0:T(8,128)}, f32[1536,768]{0,1:T(8,128)}) conditional(s32[]{:T(128)} %convert_element_type.267, () %tuple.124, (bf16[8,1536]{1,0:T(8,128)(2,1)}, bf16[8,768]{1,0:T(8,128)(2,1)S(1)}, bf16[1536,768]{1,0:T(8,128)(2,1)}, f32[8,1536]{1,0:T(8,128)S(1)}, ...), branch_computations={%region_23.24_spmd, %region_24.25_spmd} | conditional | flops 75743232 | bytes 23789600 | solution.py:50
  919.5 3.7 convolution_bitcast_fusion
  923.2 6.1 copy.106
  929.9 3.8 fusion.166
  933.9 16.5 %conditional.26 = (bf16[8,768]{1,0:T(8,128)(2,1)}, bf16[8,768]{1,0:T(8,128)(2,1)S(1)}, f32[768,1536]{1,0:T(8,128)}, f32[1536,768]{0,1:T(8,128)}) conditional(s32[]{:T(128)} %convert_element_type.267, () %tuple.136, (bf16[8,1536]{1,0:T(8,128)(2,1)}, bf16[8,768]{1,0:T(8,128)(2,1)S(1)}, bf16[1536,768]{1,0:T(8,128)(2,1)}, f32[8,1536]{1,0:T(8,128)S(1)}, ...), branch_computations={%region_44.45_spmd, %region_45.46_spmd} | conditional | flops 75743232 | bytes 23789600 | solution.py:50
  936.3 3.6 convolution_bitcast_fusion.2
  939.9 6.1 copy.110
  946.7 3.7 fusion.168
  950.4 5.9 add_convert_fusion
  956.4 5.9 add_convert_fusion.1
  964.2 7.4 all-reduce.3
  971.6 2.9 conditional.27
  974.5 2.9 conditional.21
  977.4 14.1 %all-reduce.2 = bf16[224,16]{0,1:T(8,128)(2,1)S(1)} all-reduce(bf16[224,16]{0,1:T(8,128)(2,1)S(1)} %add_convert_fusion.6), channel_id=2, replica_groups=mesh['groups'=2,'tile'=4,'segment'=2,'mp'=2] {'tile','segment'}, use_global_device_ids=true, to_apply=%region_51.52.clone | all-reduce | flops 3584 | bytes 14336
  994.1 34.7 %reduce-scatter.4.cloned.1.call-done = bf16[96,1536]{1,0:T(8,128)(2,1)} async-done(((bf16[768,1536]{1,0:T(8,128)(2,1)}), bf16[96,1536]{1,0:T(8,128)(2,1)}) %reduce-scatter.4.cloned.1.call-update) | async-done | bytes 294928 | tf_op jit(solution)/shard_map/reduce_scatter | solution.py:218
  (171 shorter events, 85.3 us)
Async XLA Ops:
  7.2 294.0 %all-gather.4.cloned.1.call-start = ((), (), s32[]{:S(2)}) async-start(), calls=%async_computation.5 | async-start | bytes 20971520 | tf_op jit(solution)/shard_map/all_gather | solution.py:70
  7.9 1.7 copy-start
  7.9 1.7 copy-start.7
  7.9 1.7 copy-start.16
  7.9 579.7 %all-gather.6.cloned.1.call-start = ((), (), s32[]{:S(2)}) async-start(), calls=%async_computation.6 | async-start | bytes 20971520 | tf_op jit(solution)/shard_map/all_gather | solution.py:71
  8.7 626.1 %all-reduce.12.cloned.1.call-start = ((), (), s32[]{:S(2)}) async-start(), calls=%async_computation.7 | async-start | bytes 1048576 | tf_op jit(solution)/shard_map/psum | solution.py:129
  10.6 3.4 copy-start.1
  16.2 3.4 copy-start.2
  20.8 10.5 %copy-start.13 = (f32[8,1536]{1,0:T(8,128)}, f32[8,1536]{1,0:T(8,128)S(1)}, u32[]{:S(2)}) copy-start(f32[8,1536]{1,0:T(8,128)S(1)} %get-tuple-element.281) | copy-start | bytes 147460
  53.6 2.2 collective-permute-start
  591.1 82.3 %all-gather.8.cloned.1.call-start = ((), (), s32[]{:S(2)}) async-start(), calls=%async_computation.8 | async-start | bytes 1966080 | tf_op jit(solution)/shard_map/all_gather | solution.py:72
  593.1 115.7 %all-reduce.14.cloned.1.call-start = ((), (), s32[]{:S(2)}) async-start(), calls=%async_computation.9 | async-start | bytes 1048576 | tf_op jit(solution)/shard_map/psum | solution.py:139
  673.6 0.8 copy-start.11
  674.4 81.2 %all-reduce.16.cloned.1.call-start = ((), (), s32[]{:S(2)}) async-start(), calls=%async_computation.10 | async-start | bytes 1048576 | tf_op jit(solution)/shard_map/psum | solution.py:148
  710.8 108.4 %all-reduce.18.cloned.1.call-start = ((), (), s32[]{:S(2)}) async-start(), calls=%async_computation.11 | async-start | bytes 1048576 | tf_op jit(solution)/shard_map/psum | solution.py:129
  768.2 3.9 collective-permute-start.1
  776.4 80.0 %all-reduce.20.cloned.1.call-start = ((), (), s32[]{:S(2)}) async-start(), calls=%async_computation.12 | async-start | bytes 1048576 | tf_op jit(solution)/shard_map/psum | solution.py:139
  821.2 0.8 copy-start.12
  822.0 81.2 %all-reduce.22.cloned.1.call-start = ((), (), s32[]{:S(2)}) async-start(), calls=%async_computation.13 | async-start | bytes 1048576 | tf_op jit(solution)/shard_map/psum | solution.py:148
  858.4 133.8 %reduce-scatter.6.cloned.1.call-start = ((), (), s32[]{:S(2)}) async-start(), calls=%async_computation.15 | async-start | bytes 2654208 | tf_op jit(solution)/shard_map/reduce_scatter | solution.py:221
  903.3 13.4 %copy-start.15 = (bf16[8,4,4,48]{3,0,1,2:T(8,128)(2,1)S(1)}, bf16[8,4,4,48]{3,0,1,2:T(8,128)(2,1)}, u32[]{:S(2)}) copy-start(bf16[8,4,4,48]{3,0,1,2:T(8,128)(2,1)} %get-tuple-element.365) | copy-start | bytes 36868
  903.3 13.5 %copy-start.14 = (f32[8,1536]{1,0:T(8,128)S(1)}, f32[8,1536]{1,0:T(8,128)}, u32[]{:S(2)}) copy-start(f32[8,1536]{1,0:T(8,128)} %copy-done.13) | copy-start | bytes 147460
  913.7 20.1 %collective-permute-start.2 = (bf16[32,4,384]{2,0,1:T(8,128)(2,1)S(1)}, bf16[32,4,384]{2,0,1:T(8,128)(2,1)S(1)}, u32[]{:S(2)}, u32[]{:S(2)}) collective-permute-start(bf16[32,4,384]{2,0,1:T(8,128)(2,1)S(1)} %bitcast.158), channel_id=1, source_target_pairs={{0,2},{2,0},{1,3},{3,1},{4,6},{6,4},{5,7},{7,5},{8,10},{10,8},{9,1... | collective-permute-start | bytes 294920 | tf_op jit(solution)/shard_map/ppermute | solution.py:8
  956.3 72.5 %reduce-scatter.4.cloned.1.call-start = ((), (), s32[]{:S(2)}) async-start(), calls=%async_computation.14 | async-start | bytes 2654208 | tf_op jit(solution)/shard_map/reduce_scatter | solution.py:218
  962.3 0.7 copy-start.19
  962.3 9.2 copy-start.8
Sparse Core Ops, SparseCore 0:
  9.6 291.5 all-gather.3
  302.7 284.9 all-gather.5
  591.2 43.4 all-reduce.11
  636.2 37.0 all-gather.7
  676.2 32.5 all-reduce.13
  711.5 44.1 all-reduce.15
  776.5 42.6 all-reduce.17
  822.2 34.1 all-reduce.19
  859.4 43.8 all-reduce.21
  956.5 34.2 reduce-scatter.5
  993.1 35.7 reduce-scatter.3
where the time goes:
time: 1050 us; the launch traced here: 1040 us
  waiting for transfers between devices  832 us (79%)
  blocking collectives  69.5 us (7%)
  local copies, waits for them, and re-layouts  49.3 us (5%)
  other arithmetic  36.6 us (3%)
  matrix products  27.4 us (3%)
  between operations  15.8 us (2%)
    all_gather x1, waiting for transfers between devices, body(): lax.all_gather(dec_out, 'tile', axis=1, tiled=True)  287 us
    all_gather x1, waiting for transfers between devices, body(): lax.all_gather(dec_in, 'tile', axis=0, tiled=True)  245 us
    psum x2, waiting for transfers between devices, teacher(): lax.psum(on_segment(later_segment, hidden_part).astype(jnp.bfloat16), 'mp')  82.4 us
    psum x2, waiting for transfers between devices, teacher(): lax.psum(partial_value.astype(jnp.bfloat16), 'mp').astype(jnp.float32)  75.1 us
    psum x2, waiting for transfers between devices, teacher(): lax.psum(on_segment(later_segment, head_part).astype(jnp.bfloat16), 'mp')  68.6 us
    all_to_all x3, blocking collectives, hand_over(): lax.all_to_all(payload, 'tile', split_axis=1, concat_axis=0, tiled=True)  38.2 us
    all_gather x1, waiting for transfers between devices, body(): lax.all_gather(head, 'tile', axis=0, tiled=True)  36.7 us
    reduce_scatter x1, waiting for transfers between devices, body(): lax.psum_scatter(in_total.astype(jnp.bfloat16), ('tile', 'segment'), scat...  34.7 us
  transfers between devices with their start and end apart: 14, of which 11 were waited for; matrix products, arithmetic and copies ran while one was open for 7% of the time, Pallas kernels for 0%

commit v1 on v0

v1 whole, which is shorter than its diff:
```python
import jax
import jax.numpy as jnp
from jax import lax
from jax.sharding import PartitionSpec as P

BF = jnp.bfloat16
F32 = jnp.float32


def inv_rms(values):
    return lax.rsqrt(jnp.mean(values * values, axis=-1, keepdims=True) + 1e-05)


def rms_back(values, gradient):
    scaling = inv_rms(values)
    normed = values * scaling
    return scaling * (gradient - normed * jnp.mean(gradient * normed, axis=-1, keepdims=True))


def gelu(v):
    return 0.5 * v * (1 + jnp.tanh(0.7978845608028654 * (v + 0.044715 * v * v * v)))


def gelu_and_slope(v):
    square = v * v
    t = jnp.tanh(0.7978845608028654 * v * (1 + 0.044715 * square))
    half = 0.5 * (1 + t)
    slope = half + 0.5 * v * (1 - t * t) * 0.7978845608028654 * (1 + 3 * 0.044715 * square)
    return v * half, slope


def dot(a, b):
    return jnp.dot(a, b, preferred_element_type=F32)


def dot_t(a, b):
    return lax.dot_general(a, b, (((1,), (1,)), ((), ())), preferred_element_type=F32)


def t_dot(a, b):
    return lax.dot_general(a, b, (((0,), (0,)), ((), ())), preferred_element_type=F32)


def body(spectra, valid, project, enc_in, enc_out, tok_embed, band_embed, dec_in, dec_out, head):
    tile, seg, mp = (lax.axis_index(a) for a in ("tile", "segment", "mp"))
    T, S, M = (lax.axis_size(a) for a in ("tile", "segment", "mp"))
    batches, per_tile, pixels, bands = spectra.shape
    codes = project.shape[1]
    width = bands // codes
    local = batches * per_tile
    share = local // (S * M)
    rows = T * local
    student = codes * pixels
    dim = tok_embed.shape[1]
    dt = dec_in.shape[0]
    hid = dec_in.shape[1] // S
    once = jnp.logical_and(seg == 0, mp == 0).astype(F32)

    patches = spectra.reshape(local, pixels, bands)
    flat = patches.reshape(local * pixels, bands)
    feat_local = (
        dot(flat, project).astype(BF).reshape(local, pixels, codes).transpose(0, 2, 1).reshape(local, student)
    )
    feats = lax.all_gather(feat_local, "tile")
    feats = feats.reshape(T, S, M, share, student).transpose(1, 2, 0, 3, 4).reshape(rows, student)
    band_all = lax.all_gather(band_embed, "tile", tiled=True)
    head_full = lax.all_gather(head, "mp", axis=1, tiled=True)

    embed = jnp.concatenate([tok_embed, band_all], axis=0)
    embed_z = lax.dynamic_slice_in_dim(embed, tile * dt, dt, 1)
    d_in = lax.dynamic_slice_in_dim(dec_in, seg * hid, hid, 1)
    d_out = lax.dynamic_slice_in_dim(dec_out, seg * hid, hid, 0)
    folded = lax.psum(dot(embed_z, d_in).astype(BF), "tile")
    fold_tok, fold_band = folded[:pixels], folded[pixels:]

    feats32 = feats.astype(F32)
    normed = (feats32 * inv_rms(feats32)).astype(BF)
    pre_act, pre_slope = gelu_and_slope(dot(normed, enc_in))
    act_out = pre_act.astype(BF)
    summed = lax.psum(dot(act_out, enc_out).astype(BF), "mp").astype(F32)
    encoded = (feats32 + summed).astype(BF)

    tokens = rows * codes
    tok = encoded.reshape(tokens, pixels)
    embedded = (
        dot(tok, tok_embed).reshape(rows, codes, dim) + band_all.astype(F32)
    ).reshape(tokens, dim).astype(BF)
    scaling = inv_rms(embedded.astype(F32))
    hid_pre = scaling * (
        dot(tok, fold_tok).reshape(rows, codes, hid) + fold_band.astype(F32)
    ).reshape(tokens, hid)
    hid_act, hid_slope = gelu_and_slope(hid_pre)
    embedded_z = lax.dynamic_slice_in_dim(embedded, tile * dt, dt, 1)
    decoded = (once * embedded_z.astype(F32) + dot(hid_act.astype(BF), d_out)).astype(BF)
    partial = dot(decoded, head_full).astype(BF)
    own = lax.psum_scatter(
        partial.reshape(S * M, T, share * codes, -1), ("segment", "mp"), scatter_dimension=0
    )
    own = lax.psum_scatter(own, "tile", scatter_dimension=0).astype(F32)
    quarter = (seg * M + mp) * share
    own_patches = lax.dynamic_slice_in_dim(patches, quarter, share, 0)
    target = (
        own_patches.reshape(share, pixels, codes, width).transpose(0, 2, 1, 3).reshape(share * codes, -1)
    )
    total_valid = jnp.sum(valid.astype(F32))
    loss_scale = 2.0 * batches * valid.shape[1] / total_valid
    own_valid = lax.dynamic_slice_in_dim(valid, tile * per_tile, per_tile, 1).reshape(local)
    own_valid = lax.dynamic_slice_in_dim(own_valid, quarter, share, 0)
    column = jnp.arange(pixels * width, dtype=jnp.int32) // width
    mask = (column[None, :] < jnp.repeat(own_valid, codes)[:, None]).astype(F32)
    grad_own = (loss_scale * mask * (own - target.astype(F32))).astype(BF)
    grad_rebuilt = lax.all_gather(
        lax.all_gather(grad_own, "tile"), ("segment", "mp")
    ).reshape(tokens, -1)

    grad_decoded = dot_t(grad_rebuilt, head_full).astype(BF)
    grad_hid = hid_slope * dot_t(grad_decoded, d_out)
    tok_z = lax.dynamic_slice_in_dim(tok_embed, tile * dt, dt, 1)
    unit_tok = dot_t((embedded.astype(F32) * scaling).astype(BF), tok_embed)
    along = jnp.sum(grad_hid * hid_pre, axis=1, keepdims=True) / dim
    grad_tok = scaling * (dot_t(grad_hid.astype(BF), fold_tok) - unit_tok * along)
    grad_tok = grad_tok + once * dot_t(grad_decoded, tok_z)
    grad_encoded = lax.psum(
        grad_tok.reshape(rows, student).astype(BF), ("tile", "segment", "mp")
    )

    grad_act = (pre_slope * dot_t(grad_encoded, enc_out)).astype(BF)
    columns = student // (T * S)
    start = (tile * S + seg) * columns
    grad_out = t_dot(act_out, lax.dynamic_slice_in_dim(grad_encoded, start, columns, 1))
    grad_in = t_dot(lax.dynamic_slice_in_dim(normed, start, columns, 1), grad_act)
    grad_normed = lax.psum(dot_t(grad_act, enc_in).astype(BF), "mp").astype(F32)
    own_rows = lambda a: lax.dynamic_slice_in_dim(
        a.reshape(S * M, T, share, student), tile, 1, 1
    ).reshape(local, student)
    grad_feat = (
        own_rows(grad_encoded).astype(F32) + rms_back(feat_local.astype(F32), own_rows(grad_normed))
    ).astype(BF)
    grad_codes = grad_feat.reshape(local, codes, pixels).transpose(0, 2, 1).reshape(-1, codes)
    grad_proj = jnp.sum(lax.all_gather(t_dot(flat, grad_codes), "tile"), axis=0)
    proj_rows = bands // (T * S)
    grad_proj = lax.dynamic_slice_in_dim(grad_proj, (tile * S + seg) * proj_rows, proj_rows, 0)
    return (grad_proj, grad_in, grad_out)


def solution(mesh):
    placed = (
        P(None, ("groups", "tile"), None, None),
        P(None, "groups"),
        P(),
        P(None, "mp"),
        P("mp", None),
        P(),
        P("tile", None),
        P("tile", "mp"),
        P("mp", "tile"),
        P("tile", "mp"),
    )
    return jax.shard_map(
        body,
        mesh=mesh,
        in_specs=placed,
        out_specs=(
            P(("groups", "tile", "segment"), None),
            P(("groups", "tile", "segment"), "mp"),
            P(("groups", "mp"), ("tile", "segment")),
        ),
        check_vma=False,
    )
```

time: 1050 us -> 351 us (0.33); the launches traced: 1040 us -> 350 us
  waiting for transfers between devices: 832 us -> 195 us
  local copies, waits for them, and re-layouts: 49.3 us -> 15.7 us
  other arithmetic: 36.6 us -> 12.3 us
  matrix products: 27.4 us -> 45.8 us
    all_gather x3 -> x1, waiting for transfers between devices: 569 us -> 17.2 us  [body(): lax.all_gather(lax.all_gather(grad_own, 'tile'), ('segment', 'mp'))]
    psum x6 -> x4, waiting for transfers between devices: 226 us -> 133 us  [the longest x1 86.1 us: body(): lax.psum(grad_tok.reshape(rows, student).astype(BF), ('tile', 'segment',...]
    all_gather x0 -> x5, blocking collectives: none -> 65.8 us  [the longest x1 15.8 us: body(): lax.all_gather(grad_own, 'tile')]
    all_to_all x3 -> x0, blocking collectives: 38.2 us -> none  [hand_over(): lax.all_to_all(payload, 'tile', split_axis=1, concat_axis=0, tiled=True)]
    dot_general x14 -> x17, matrix products: 19.9 us -> 45.8 us  [the longest x7 21.1 us: dot(): return jnp.dot(a, b, preferred_element_type=F32)]
    convert_element_type x20 -> x9, other arithmetic: 30.6 us -> 9.57 us  [the longest x1 5.29 us: body(): hid_act.astype(BF)]
    psum x2 -> x0, blocking collectives: 17.1 us -> none  [the longest x1 9.73 us: student_forward(): lax.psum(partial_value.astype(jnp.bfloat16), 'mp').astype(jnp.float32)]
    unnamed x1 -> x0, blocking collectives: 14.1 us -> none
  transfers between devices with their start and end apart: 14 -> 7, of which waited for: 11 -> 6; matrix products, arithmetic and copies ran while one was open for 7% -> 5% of each run, Pallas kernels for 0% -> 0%
where the time goes in v1:
time: 351 us; the launch traced here: 350 us
  waiting for transfers between devices  195 us (56%)
  blocking collectives  65.8 us (19%)
  matrix products  45.8 us (13%)
  local copies, waits for them, and re-layouts  15.7 us (4%)
  between operations  15.2 us (4%)
  other arithmetic  12.3 us (4%)
    psum x1, waiting for transfers between devices, body(): lax.psum(grad_tok.reshape(rows, student).astype(BF), ('tile', 'segment',...  86.1 us
    psum x1, waiting for transfers between devices, body(): folded = lax.psum(dot(embed_z, d_in).astype(BF), 'tile')  29.6 us
    reduce_scatter x1, waiting for transfers between devices, body(): lax.psum_scatter(partial.reshape(S * M, T, share * codes, -1), ('segment'...  28 us
    dot_general x7, matrix products, dot(): return jnp.dot(a, b, preferred_element_type=F32)  21.1 us
    dot_general x7, matrix products, dot_t(): lax.dot_general(a, b, (((1,), (1,)), ((), ())), preferred_element_type=F32)  20.7 us
    all_gather x1, waiting for transfers between devices, body(): lax.all_gather(lax.all_gather(grad_own, 'tile'), ('segment', 'mp'))  17.2 us
    psum x1, waiting for transfers between devices, body(): grad_normed = lax.psum(dot_t(grad_act, enc_in).astype(BF), 'mp').astype(F32)  17.2 us
    reduce_scatter x1, waiting for transfers between devices, body(): own = lax.psum_scatter(own, 'tile', scatter_dimension=0).astype(F32)  17 us
  transfers between devices with their start and end apart: 7, of which 6 were waited for; matrix products, arithmetic and copies ran while one was open for 5% of the time, Pallas kernels for 0%

profile of v1, /device:TPU:0, one launch (start us, length us, event | category | flops | bytes accessed | tf_op | source)
XLA Modules:
  0.0 350.5 jit_solution(10092934858017082224)
XLA Ops:
  7.2 1.4 convolution_convert_fusion.5
  9.6 15.0 %all_gather.25 = bf16[4,16,768]{2,1,0:T(8,128)(2,1)S(1)} all-gather(bf16[1,16,768]{2,1,0:T(8,128)(2,1)S(1)} %all_gather_reshape.3), channel_id=1, replica_groups=mesh['groups'=2,'tile'=4,'segment'=2,'mp'=2] {'tile'}, dimensions={0}, use_global_device_ids=true | all-gather | bytes 122880 | tf_op jit(solution)/shard_map/all_gather | solution.py:64
  25.2 2.2 fusion.50
  28.2 1.2 convolution_convert_fusion.4
  29.5 13.3 %all-gather.2 = bf16[4,4,2048]{2,1,0:T(4,128)(2,1)S(1)} all-gather(bf16[1,4,2048]{2,1,0:T(4,128)(2,1)S(1)} %bitcast.88), channel_id=1, replica_groups=mesh['groups'=2,'tile'=4,'segment'=2,'mp'=2] {'tile'}, dimensions={0}, use_global_device_ids=true | all-gather | bytes 81920 | tf_op jit(solution)/shard_map/all_gather | solution.py:66
  42.8 2.8 convolution_convert_fusion
  46.4 8.4 %all_gather.27 = bf16[512,672]{0,1:T(8,128)(2,1)S(1)} all-gather(bf16[512,336]{0,1:T(8,128)(2,1)} %param.19), channel_id=1, replica_groups=mesh['groups'=2,'tile'=4,'segment'=2,'mp'=2] {'mp'}, dimensions={1}, use_global_device_ids=true | all-gather | bytes 1032192 | tf_op jit(solution)/shard_map/all_gather | solution.py:67
  56.1 4.2 %multiply_reduce_fusion.1 = (f32[64,16]{1,0:T(8,128)S(1)}, bf16[64,16,2048]{2,1,0:T(8,128)(2,1)}) fusion(f32[16,2048]{1,0:T(8,128)} %convert_element_type.165, bf16[64,16,48]{2,1,0:T(8,128)(2,1)S(1)} %dot_general.61, bf16[48,2048]{1,0:T(8,128)(2,1)} %param.15), kind=kOutput, calls=%fused_computation.7 | convolution fusion | flops 211811328 | bytes 4624384 | tf_op jit(solution)/shard_map/dot_general | solution.py:33
  60.4 29.6 %all-reduce.7.cloned.1.call-done = bf16[64,2048]{1,0:T(8,128)(2,1)} async-done(((bf16[64,2048]{1,0:T(8,128)(2,1)}), bf16[64,2048]{1,0:T(8,128)(2,1)}) %all-reduce.7.cloned.1.call-update) | async-done | bytes 262160 | tf_op jit(solution)/shard_map/psum | solution.py:73
  90.8 2.2 convolution_add_fusion
  93.0 5.3 %multiply_convert_fusion.1 = bf16[1024,2048]{1,0:T(8,128)(2,1)} fusion(f32[64,16,2048]{2,1,0:T(8,128)S(1)} %convolution_add_fusion, f32[1024]{0:T(1024)S(1)} %rsqrt.37), kind=kLoop, calls=%fused_computation.3 | loop fusion | flops 20971520 | bytes 12587008 | tf_op jit(solution)/shard_map/convert_element_type | solution.py:94
  98.3 7.2 %convolution_convert_fusion.1 = bf16[1024,672]{0,1:T(8,128)(2,1)} fusion(bf16[512,672]{0,1:T(8,128)(2,1)S(1)} %all_gather.27, bf16[1024,2048]{1,0:T(8,128)(2,1)} %multiply_convert_fusion.1, bf16[4096,512]{1,0:T(8,128)(2,1)} %param.18, s32[]{:T(128)S(6)} %select_n.37, bf16[1024,2048]{1,0:T(8,128)(2,1)} %bitcast.90, s32[]{:T(128)S(6)} %select_n.36, ...), kind=kOutput, calls=%fused_computation.22 | convolution fusion | flops 2854912000 | bytes 9404428 | tf_op jit(solution)/shard_map/dot_general | solution.py:33
  105.5 2.6 copy.40
  108.2 28.0 %reduce-scatter.3.cloned.1.call-done = bf16[1,4,64,672]{3,2,1,0:T(8,128)(2,1)} async-done(((bf16[4,4,64,672]{3,2,1,0:T(8,128)(2,1)}), bf16[1,4,64,672]{3,2,1,0:T(8,128)(2,1)}) %reduce-scatter.3.cloned.1.call-update) | async-done | bytes 344080 | tf_op jit(solution)/shard_map/reduce_scatter | solution.py:96
  136.9 1.8 copy.42
  138.7 1.9 reshape.268
  142.0 17.0 %reduce-scatter.5.cloned.1.call-done = bf16[1,64,672]{2,1,0:T(8,128)(2,1)} async-done(((bf16[4,64,672]{2,1,0:T(8,128)(2,1)}), bf16[1,64,672]{2,1,0:T(8,128)(2,1)}) %reduce-scatter.5.cloned.1.call-update) | async-done | bytes 86032 | tf_op jit(solution)/shard_map/reduce_scatter | solution.py:99
  160.0 15.8 %all_gather.28 = bf16[4,64,672]{2,1,0:T(8,128)(2,1)} all-gather(bf16[1,64,672]{2,1,0:T(8,128)(2,1)S(1)} %multiply_convert_fusion.6), channel_id=1, replica_groups=mesh['groups'=2,'tile'=4,'segment'=2,'mp'=2] {'tile'}, dimensions={0}, use_global_device_ids=true | all-gather | bytes 430080 | tf_op jit(solution)/shard_map/all_gather | solution.py:113
  176.2 17.2 %all-gather.6.cloned.1.call-done = bf16[16,64,672]{2,1,0:T(8,128)(2,1)} async-done(((bf16[4,64,672]{2,1,0:T(8,128)(2,1)}), bf16[16,64,672]{2,1,0:T(8,128)(2,1)}) %all-gather.6.cloned.1.call-update) | async-done | bytes 1376272 | tf_op jit(solution)/shard_map/all_gather | solution.py:112
  193.4 2.7 convolution_convert_fusion.2
  196.3 9.2 %multiply_reduce_fusion = (f32[1024]{0:T(1024)S(1)}, bf16[1024,2048]{1,0:T(8,128)(2,1)S(1)}) fusion(f32[64,16,2048]{2,1,0:T(8,128)} %copy-done.1, f32[1024]{0:T(1024)S(1)} %rsqrt.37, bf16[1024,512]{1,0:T(8,128)(2,1)S(1)} %convolution_convert_fusion.2, bf16[4096,512]{1,0:T(8,128)(2,1)S(1)} %copy-done.12, s32[]{:T(128)S(6)} %select_n.37), kind=kOutput, calls=%fused_computation.1 | convolution fusion | flops 2191522816 | bytes 15736836 | tf_op jit(solution)/shard_map/dot_general | solution.py:37
  206.0 1.5 fusion.20
  207.5 2.0 fusion.21
  209.5 1.1 copy.43
  211.6 1.0 reshape.270
  212.7 86.1 %all-reduce.9.cloned.1.call-done = bf16[64,768]{1,0:T(8,128)(2,1)} async-done(((bf16[64,768]{1,0:T(8,128)(2,1)}), bf16[64,768]{1,0:T(8,128)(2,1)}) %all-reduce.9.cloned.1.call-update) | async-done | bytes 98320 | tf_op jit(solution)/shard_map/psum | solution.py:123
  298.8 1.7 fusion.4
  300.5 3.1 convolution_convert_fusion.3
  303.7 1.9 fusion.36
  307.2 1.9 fusion.34
  310.2 17.2 %all-reduce.11.cloned.1.call-done = bf16[4,4,4,768]{3,2,0,1:T(4,128)(2,1)} async-done(((bf16[4,4,4,768]{3,2,0,1:T(4,128)(2,1)}), bf16[4,4,4,768]{3,2,0,1:T(4,128)(2,1)}) %all-reduce.11.cloned.1.call-update) | async-done | bytes 98320 | tf_op jit(solution)/shard_map/psum | solution.py:132
  329.7 13.3 %all-gather.3 = f32[4,224,16]{1,2,0:T(8,128)S(1)} all-gather(f32[1,224,16]{1,2,0:T(8,128)S(1)} %convolution_bitcast_fusion), channel_id=3, replica_groups=mesh['groups'=2,'tile'=4,'segment'=2,'mp'=2] {'tile'}, dimensions={0}, use_global_device_ids=true | all-gather | bytes 71680 | tf_op jit(solution)/shard_map/all_gather | solution.py:140
  (94 shorter events, 15.4 us)
Async XLA Ops:
  7.2 21.0 %copy-start = (bf16[1536,768]{1,0:T(8,128)(2,1)S(1)}, bf16[1536,768]{1,0:T(8,128)(2,1)}, u32[]{:S(2)}) copy-start(bf16[1536,768]{1,0:T(8,128)(2,1)} %param.14) | copy-start | bytes 7077892
  7.2 22.3 %copy-start.10 = (bf16[4,2048]{1,0:T(4,128)(2,1)S(1)}, bf16[4,2048]{1,0:T(4,128)(2,1)}, u32[]{:S(2)}) copy-start(bf16[4,2048]{1,0:T(4,128)(2,1)} %param.16) | copy-start | bytes 49156
  7.2 47.6 %all-reduce.5.cloned.1.call-start = ((), (), s32[]{:S(2)}) async-start(), calls=%async_computation.2 | async-start | bytes 196608 | tf_op jit(solution)/shard_map/psum | solution.py:80
  7.2 35.6 %copy-start.8 = (bf16[48,2048]{1,0:T(8,128)(2,1)S(1)}, bf16[48,2048]{1,0:T(8,128)(2,1)}, u32[]{:S(2)}) copy-start(bf16[48,2048]{1,0:T(8,128)(2,1)} %param.15) | copy-start | bytes 589828
  25.2 4.3 %copy-start.7 = (bf16[64,768]{1,0:T(8,128)(2,1)}, bf16[64,768]{1,0:T(8,128)(2,1)S(1)}, u32[]{:S(2)}) copy-start(bf16[64,768]{1,0:T(8,128)(2,1)S(1)} %multiply_convert_fusion.7) | copy-start | bytes 294916
  27.4 0.8 copy-start.3
  29.4 60.6 %all-reduce.7.cloned.1.call-start = ((), (), s32[]{:S(2)}) async-start(), calls=%async_computation.3 | async-start | bytes 524288 | tf_op jit(solution)/shard_map/psum | solution.py:73
  45.6 90.6 %reduce-scatter.3.cloned.1.call-start = ((), (), s32[]{:S(2)}) async-start(), calls=%async_computation.4 | async-start | bytes 1966080 | tf_op jit(solution)/shard_map/reduce_scatter | solution.py:96
  54.7 43.5 %copy-start.6 = (bf16[512,672]{0,1:T(8,128)(2,1)}, bf16[512,672]{0,1:T(8,128)(2,1)S(1)}, u32[]{:S(2)}) copy-start(bf16[512,672]{0,1:T(8,128)(2,1)S(1)} %all_gather.27) | copy-start | bytes 2064388
  93.0 5.3 %copy-start.1 = (f32[64,16,2048]{2,1,0:T(8,128)}, f32[64,16,2048]{2,1,0:T(8,128)S(1)}, u32[]{:S(2)}) copy-start(f32[64,16,2048]{2,1,0:T(8,128)S(1)} %convolution_add_fusion) | copy-start | bytes 25165828
  105.5 30.8 %copy-start.11 = (s32[2,32]{1,0:T(2,128)S(1)}, s32[2,32]{1,0:T(2,128)}, u32[]{:S(2)}) copy-start(s32[2,32]{1,0:T(2,128)} %param.11) | copy-start | bytes 772
  105.5 31.2 %copy-start.2 = (bf16[2,8,48,224]{3,2,1,0:T(8,128)(2,1)S(1)}, bf16[2,8,48,224]{3,2,1,0:T(8,128)(2,1)}, u32[]{:S(2)}) copy-start(bf16[2,8,48,224]{3,2,1,0:T(8,128)(2,1)} %param.10) | copy-start | bytes 1032196
  108.1 50.8 %reduce-scatter.5.cloned.1.call-start = ((), (), s32[]{:S(2)}) async-start(), calls=%async_computation.5 | async-start | bytes 491520 | tf_op jit(solution)/shard_map/reduce_scatter | solution.py:99
  136.2 57.2 %all-gather.6.cloned.1.call-start = ((), (), s32[]{:S(2)}) async-start(), calls=%async_computation.8 | async-start | bytes 1966080 | tf_op jit(solution)/shard_map/all_gather | solution.py:112
  175.8 123.0 %all-reduce.9.cloned.1.call-start = ((), (), s32[]{:S(2)}) async-start(), calls=%async_computation.6 | async-start | bytes 196608 | tf_op jit(solution)/shard_map/psum | solution.py:123
  193.4 2.9 copy-start.12
  196.3 9.2 %copy-start.9 = (bf16[48,2048]{1,0:T(8,128)(2,1)S(1)}, bf16[48,2048]{1,0:T(8,128)(2,1)}, u32[]{:S(2)}) copy-start(bf16[48,2048]{1,0:T(8,128)(2,1)} %param.15) | copy-start | bytes 589828
  196.3 9.7 %copy-start.13 = (bf16[64,16,2048]{2,1,0:T(8,128)(2,1)S(1)}, bf16[64,16,2048]{2,1,0:T(8,128)(2,1)}, u32[]{:S(2)}) copy-start(bf16[64,16,2048]{2,1,0:T(8,128)(2,1)} %get-tuple-element.6) | copy-start | bytes 12582916
  206.0 1.5 copy-start.5
  207.5 91.4 %copy-start.4 = (f32[64,1536]{1,0:T(8,128)S(1)}, f32[64,1536]{1,0:T(8,128)}, u32[]{:S(2)}) copy-start(f32[64,1536]{1,0:T(8,128)} %copy-done.3) | copy-start | bytes 1179652
  211.5 115.9 %all-reduce.11.cloned.1.call-start = ((), (), s32[]{:S(2)}) async-start(), calls=%async_computation.7 | async-start | bytes 196608 | tf_op jit(solution)/shard_map/psum | solution.py:132
Sparse Core Ops, SparseCore 0:
  29.5 22.1 all-reduce.4
  54.6 35.3 all-reduce.6
  108.3 27.9 reduce-scatter.2
  138.3 20.5 reduce-scatter.4
  175.9 17.4 all-gather.5
  211.6 87.1 all-reduce.8
  307.3 20.0 all-reduce.10

commit v2 on v1

--- a/solution.py
+++ b/solution.py
@@ -1,6 +1,8 @@
 import jax
 import jax.numpy as jnp
 from jax import lax
+from jax.experimental import pallas as pl
+from jax.experimental.pallas import tpu as pltpu
 from jax.sharding import PartitionSpec as P
 
 BF = jnp.bfloat16
@@ -39,6 +41,259 @@
 
 def t_dot(a, b):
     return lax.dot_general(a, b, (((0,), (0,)), ((), ())), preferred_element_type=F32)
+
+
+MESH = pl.DeviceIdType.MESH
+DMA = pltpu.SemaphoreType.DMA
+
+
+def shifted(axis, step):
+    return lax.rem(lax.axis_index(axis) + step, lax.axis_size(axis))
+
+
+def greet(peers):
+    barrier = pltpu.get_barrier_semaphore()
+    for peer in peers:
+        pl.semaphore_signal(barrier, inc=1, device_id=peer, device_id_type=MESH)
+    pl.semaphore_wait(barrier, len(peers))
+
+
+def ring(axis):
+    return [{axis: shifted(axis, k)} for k in range(1, lax.axis_size(axis))]
+
+
+def push(src, dst, send, recv, peer):
+    copy = pltpu.make_async_remote_copy(
+        src_ref=src, dst_ref=dst, send_sem=send, recv_sem=recv, device_id=peer, device_id_type=MESH
+    )
+    copy.start()
+    return copy
+
+
+def finish(copies):
+    for copy in copies:
+        copy.wait_recv()
+
+
+def vmem_call(kernel, name, number, outs, scratch, *args):
+    return pl.pallas_call(
+        kernel,
+        out_shape=outs,
+        in_specs=[pl.BlockSpec(memory_space=pltpu.VMEM)] * len(args),
+        out_specs=jax.tree.map(lambda _: pl.BlockSpec(memory_space=pltpu.VMEM), outs),
+        scratch_shapes=scratch,
+        compiler_params=pltpu.CompilerParams(
+            collective_id=number, has_side_effects=True, vmem_limit_bytes=56 << 20
+        ),
+        name=name,
+    )(*args)
+
+
+def gather_tile(feat, band):
+    count = lax.axis_size("tile")
+
+    def kernel(feat_ref, band_ref, feats_ref, bands_ref, send, recv):
+        me = lax.axis_index("tile")
+        peers = ring("tile")
+        greet(peers)
+        copies = []
+        for k, peer in enumerate(peers):
+            copies.append(push(feat_ref, feats_ref.at[me], send.at[0, k], recv.at[0, k], peer))
+            copies.append(push(band_ref, bands_ref.at[me], send.at[1, k], recv.at[1, k], peer))
+        feats_ref[me] = feat_ref[...]
+        bands_ref[me] = band_ref[...]
+        for copy in copies:
+            copy.wait()
+
+    outs = [jax.ShapeDtypeStruct((count,) + a.shape, a.dtype) for a in (feat, band)]
+    return vmem_call(kernel, "gather_tile", 0, outs, [DMA((2, count - 1))] * 2, feat, band)
+
+
+def fold_exchange(fold, part, head):
+    T, M = lax.axis_size("tile"), lax.axis_size("mp")
+
+    def kernel(fold_ref, part_ref, head_ref, sum_ref, parts_ref, heads_ref, slots, send, recv, xsend, xrecv):
+        me, mine = lax.axis_index("tile"), lax.axis_index("mp")
+        tiles, mps = ring("tile"), ring("mp")
+        greet(tiles + mps)
+        first = []
+        for k, peer in enumerate(tiles):
+            first.append(push(fold_ref.at[peer["tile"]], slots.at[k], send.at[0, k], recv.at[0, k], peer))
+        across = []
+        for k, peer in enumerate(mps):
+            across.append(push(part_ref, parts_ref.at[mine], xsend.at[0, k], xrecv.at[0, k], peer))
+            across.append(push(head_ref, heads_ref.at[mine], xsend.at[1, k], xrecv.at[1, k], peer))
+        parts_ref[mine] = part_ref[...]
+        heads_ref[mine] = head_ref[...]
+        finish(first)
+        total = fold_ref[me].astype(F32)
+        for k in range(T - 1):
+            total = total + slots[k].astype(F32)
+        sum_ref[me] = total.astype(BF)
+        second = []
+        for k, peer in enumerate(tiles):
+            second.append(push(sum_ref.at[me], sum_ref.at[me], send.at[1, k], recv.at[1, k], peer))
+        finish(second + across)
+        for copy in first + second + across:
+            copy.wait_send()
+
+    outs = [
+        jax.ShapeDtypeStruct(fold.shape, BF),
+        jax.ShapeDtypeStruct((M,) + part.shape, BF),
+        jax.ShapeDtypeStruct((M,) + head.shape, BF),
+    ]
+    scratch = [pltpu.VMEM((T - 1,) + fold.shape[1:], BF)] + [DMA((2, T - 1))] * 2 + [DMA((2, M - 1))] * 2
+    return vmem_call(kernel, "fold_exchange", 1, outs, scratch, fold, part, head)
+
+
+def rebuilt_exchange(part, target, factor):
+    C, S, M, T, q, R = part.shape
+    most = max(S, M, T) - 1
+
+    def kernel(part_ref, target_ref, factor_ref, grad_ref, s_in, s_sum, m_in, m_sum, t_in, send, recv):
+        s, m, t = (lax.axis_index(a) for a in ("segment", "mp", "tile"))
+        segs, mps, tiles = ring("segment"), ring("mp"), ring("tile")
+        greet(segs + mps + tiles)
+        live = [None] * C
+        everything = []
+
+        def launch(c, stage, peers, source, landing):
+            live[c] = [
+                push(source(k, p), landing(k), send.at[stage, c, k], recv.at[stage, c, k], p)
+                for k, p in enumerate(peers)
+            ]
+            everything.extend(live[c])
+
+        def advance(c, stage):
+            if stage > 0:
+                finish(live[c])
+            if stage == 0:
+                launch(c, 0, segs, lambda k, p: part_ref.at[c, p["segment"]], lambda k: s_in.at[c, k])
+            if stage == 1:
+                for other in range(M):
+                    total = part_ref[c, s, other].astype(F32)
+                    for k in range(S - 1):
+                        total = total + s_in[c, k, other].astype(F32)
+                    s_sum[c, other] = total.astype(BF)
+                launch(c, 1, mps, lambda k, p: s_sum.at[c, p["mp"]], lambda k: m_in.at[c, k])
+            if stage == 2:
+                total = s_sum[c, m].astype(F32)
+                for k in range(M - 1):
+                    total = total + m_in[c, k].astype(F32)
+                m_sum[c] = total.astype(BF)
+                launch(c, 2, tiles, lambda k, p: m_sum.at[c, p["tile"]], lambda k: t_in.at[c, k])
+            if stage == 3:
+                total = m_sum[c, t].astype(F32)
+                for k in range(T - 1):
+                    total = total + t_in[c, k].astype(F32)
+                grad = factor_ref[c] * (total - target_ref[c].astype(F32))
+                grad_ref[c, s, m, t] = grad.astype(BF)
+                own = grad_ref.at[c, s, m, t]
+                launch(c, 3, tiles, lambda k, p: own, lambda k: own)
+            if stage == 4:
+                own = grad_ref.at[c, s, m]
+                launch(c, 4, mps, lambda k, p: own, lambda k: own)
+            if stage == 5:
+                own = grad_ref.at[c, s]
+                launch(c, 5, segs, lambda k, p: own, lambda k: own)
+
+        for step in range(7 + C - 1):
+            for c in range(C):
+                if 0 <= step - c <= 6:
+                    advance(c, step - c)
+        for copy in everything:
+            copy.wait_send()
+
+    scratch = [
+        pltpu.VMEM((C, S - 1, M, T, q, R), BF),
+        pltpu.VMEM((C, M, T, q, R), BF),
+        pltpu.VMEM((C, M - 1, T, q, R), BF),
+        pltpu.VMEM((C, T, q, R), BF),
+        pltpu.VMEM((C, T - 1, q, R), BF),
+        DMA((6, C, most)),
+        DMA((6, C, most)),
+    ]
+    return vmem_call(
+        kernel, "rebuilt_exchange", 2, jax.ShapeDtypeStruct(part.shape, BF), scratch, part, target, factor
+    )
+
+
+def token_sum(part):
+    T, rows, width = part.shape
+    S, M = lax.axis_size("segment"), lax.axis_size("mp")
+    most = max(S, M, T) - 1
+
+    def kernel(part_ref, sum_ref, s_in, s_sum, m_in, m_sum, t_in, send, recv):
+        t = lax.axis_index("tile")
+        segs, mps, tiles = ring("segment"), ring("mp"), ring("tile")
+        greet(segs + mps + tiles)
+        everything = []
+
+        def launch(stage, peers, source, landing):
+            copies = [
+                push(source(p), landing(k), send.at[stage, k], recv.at[stage, k], p)
+                for k, p in enumerate(peers)
+            ]
+            everything.extend(copies)
+            finish(copies)
+
+        launch(0, segs, lambda p: part_ref, lambda k: s_in.at[k])
+        total = part_ref[...].astype(F32)
+        for k in range(S - 1):
+            total = total + s_in[k].astype(F32)
+        s_sum[...] = total.astype(BF)
+        launch(1, mps, lambda p: s_sum, lambda k: m_in.at[k])
+        total = s_sum[...].astype(F32)
+        for k in range(M - 1):
+            total = total + m_in[k].astype(F32)
+        m_sum[...] = total.astype(BF)
+        launch(2, tiles, lambda p: m_sum.at[p["tile"]], lambda k: t_in.at[k])
+        total = m_sum[t].astype(F32)
+        for k in range(T - 1):
+            total = total + t_in[k].astype(F32)
+        sum_ref[t] = total.astype(BF)
+        own = sum_ref.at[t]
+        launch(3, tiles, lambda p: own, lambda k: own)
+        for copy in everything:
+            copy.wait_send()
+
+    scratch = [
+        pltpu.VMEM((S - 1,) + part.shape, BF),
+        pltpu.VMEM(part.shape, BF),
+        pltpu.VMEM((M - 1,) + part.shape, BF),
+        pltpu.VMEM(part.shape, BF),
+        pltpu.VMEM((T - 1, rows, width), BF),
+        DMA((4, most)),
+        DMA((4, most)),
+    ]
+    return vmem_call(kernel, "token_sum", 3, jax.ShapeDtypeStruct(part.shape, BF), scratch, part)
+
+
+def project_sum(part):
+    T, S, M = (lax.axis_size(a) for a in ("tile", "segment", "mp"))
+    count = T * M
+
+    def kernel(part_ref, sum_ref, slots, send, recv):
+        s, t = lax.axis_index("segment"), lax.axis_index("tile")
+        peers = [
+            {"tile": shifted("tile", k // M), "mp": shifted("mp", k % M)} for k in range(1, count)
+        ]
+        greet(peers)
+        copies = []
+        for k, peer in enumerate(peers):
+            copies.append(
+                push(part_ref.at[peer["tile"] * S + s], slots.at[k], send.at[k], recv.at[k], peer)
+            )
+        finish(copies)
+        total = part_ref[t * S + s]
+        for k in range(count - 1):
+            total = total + slots[k]
+        sum_ref[...] = total
+        for copy in copies:
+            copy.wait_send()
+
+    scratch = [pltpu.VMEM((count - 1,) + part.shape[1:], F32), DMA((count - 1,)), DMA((count - 1,))]
+    return vmem_call(kernel, "project_sum", 4, jax.ShapeDtypeStruct(part.shape[1:], F32), scratch, part)
 
 
 def body(spectra, valid, project, enc_in, enc_out, tok_embed, band_embed, dec_in, dec_out, head):
@@ -49,6 +304,8 @@
     width = bands // codes
     local = batches * per_tile
     share = local // (S * M)
+    parts = 2 if share % 2 == 0 else 1
+    piece = share // parts
     rows = T * local
     student = codes * pixels
     dim = tok_embed.shape[1]
@@ -61,23 +318,27 @@
     feat_local = (
         dot(flat, project).astype(BF).reshape(local, pixels, codes).transpose(0, 2, 1).reshape(local, student)
     )
-    feats = lax.all_gather(feat_local, "tile")
-    feats = feats.reshape(T, S, M, share, student).transpose(1, 2, 0, 3, 4).reshape(rows, student)
-    band_all = lax.all_gather(band_embed, "tile", tiled=True)
-    head_full = lax.all_gather(head, "mp", axis=1, tiled=True)
+    feats, band_all = gather_tile(feat_local, band_embed)
+    feats = (
+        feats.reshape(T, parts, S, M, piece, student).transpose(1, 2, 3, 0, 4, 5).reshape(rows, student)
+    )
+    band_all = band_all.reshape(codes, dim)
 
     embed = jnp.concatenate([tok_embed, band_all], axis=0)
     embed_z = lax.dynamic_slice_in_dim(embed, tile * dt, dt, 1)
     d_in = lax.dynamic_slice_in_dim(dec_in, seg * hid, hid, 1)
     d_out = lax.dynamic_slice_in_dim(dec_out, seg * hid, hid, 0)
-    folded = lax.psum(dot(embed_z, d_in).astype(BF), "tile")
-    fold_tok, fold_band = folded[:pixels], folded[pixels:]
+    fold_part = dot(embed_z, d_in).astype(BF).reshape(-1, T, hid // T).transpose(1, 0, 2)
 
     feats32 = feats.astype(F32)
     normed = (feats32 * inv_rms(feats32)).astype(BF)
     pre_act, pre_slope = gelu_and_slope(dot(normed, enc_in))
     act_out = pre_act.astype(BF)
-    summed = lax.psum(dot(act_out, enc_out).astype(BF), "mp").astype(F32)
+    folded, summed, heads = fold_exchange(fold_part, dot(act_out, enc_out).astype(BF), head)
+    folded = folded.transpose(1, 0, 2).reshape(-1, hid)
+    fold_tok, fold_band = folded[:pixels], folded[pixels:]
+    head_full = heads.transpose(1, 0, 2).reshape(dt, -1)
+    summed = jnp.sum(summed.astype(F32), axis=0)
     encoded = (feats32 + summed).astype(BF)
 
     tokens = rows * codes
@@ -93,24 +354,28 @@
     embedded_z = lax.dynamic_slice_in_dim(embedded, tile * dt, dt, 1)
     decoded = (once * embedded_z.astype(F32) + dot(hid_act.astype(BF), d_out)).astype(BF)
     partial = dot(decoded, head_full).astype(BF)
-    own = lax.psum_scatter(
-        partial.reshape(S * M, T, share * codes, -1), ("segment", "mp"), scatter_dimension=0
-    )
-    own = lax.psum_scatter(own, "tile", scatter_dimension=0).astype(F32)
-    quarter = (seg * M + mp) * share
-    own_patches = lax.dynamic_slice_in_dim(patches, quarter, share, 0)
+    place = (seg * M + mp) * piece
+
+    def mine(a):
+        a = a.reshape((parts, S * M * piece) + a.shape[1:])
+        a = lax.dynamic_slice_in_dim(a, place, piece, 1)
+        return a.reshape((share,) + a.shape[2:])
+
+    own_patches = mine(patches)
     target = (
         own_patches.reshape(share, pixels, codes, width).transpose(0, 2, 1, 3).reshape(share * codes, -1)
     )
     total_valid = jnp.sum(valid.astype(F32))
     loss_scale = 2.0 * batches * valid.shape[1] / total_valid
     own_valid = lax.dynamic_slice_in_dim(valid, tile * per_tile, per_tile, 1).reshape(local)
-    own_valid = lax.dynamic_slice_in_dim(own_valid, quarter, share, 0)
+    own_valid = mine(own_valid)
     column = jnp.arange(pixels * width, dtype=jnp.int32) // width
     mask = (column[None, :] < jnp.repeat(own_valid, codes)[:, None]).astype(F32)
-    grad_own = (loss_scale * mask * (own - target.astype(F32))).astype(BF)
-    grad_rebuilt = lax.all_gather(
-        lax.all_gather(grad_own, "tile"), ("segment", "mp")
+    block = (parts, piece * codes, pixels * width)
+    grad_rebuilt = rebuilt_exchange(
+        partial.reshape(parts, S, M, T, piece * codes, -1),
+        target.reshape(block),
+        (loss_scale * mask).reshape(block),
     ).reshape(tokens, -1)
 
     grad_decoded = dot_t(grad_rebuilt, head_full).astype(BF)
@@ -120,26 +385,23 @@
     along = jnp.sum(grad_hid * hid_pre, axis=1, keepdims=True) / dim
     grad_tok = scaling * (dot_t(grad_hid.astype(BF), fold_tok) - unit_tok * along)
     grad_tok = grad_tok + once * dot_t(grad_decoded, tok_z)
-    grad_encoded = lax.psum(
-        grad_tok.reshape(rows, student).astype(BF), ("tile", "segment", "mp")
-    )
+    grad_encoded = token_sum(grad_tok.reshape(T, local, student).astype(BF)).reshape(rows, student)
 
     grad_act = (pre_slope * dot_t(grad_encoded, enc_out)).astype(BF)
     columns = student // (T * S)
     start = (tile * S + seg) * columns
     grad_out = t_dot(act_out, lax.dynamic_slice_in_dim(grad_encoded, start, columns, 1))
     grad_in = t_dot(lax.dynamic_slice_in_dim(normed, start, columns, 1), grad_act)
-    grad_normed = lax.psum(dot_t(grad_act, enc_in).astype(BF), "mp").astype(F32)
     own_rows = lambda a: lax.dynamic_slice_in_dim(
-        a.reshape(S * M, T, share, student), tile, 1, 1
+        a.reshape(parts * S * M, T, piece, student), tile, 1, 1
     ).reshape(local, student)
+    grad_normed = own_rows(dot_t(grad_act, enc_in).astype(BF)).astype(F32)
     grad_feat = (
-        own_rows(grad_encoded).astype(F32) + rms_back(feat_local.astype(F32), own_rows(grad_normed))
+        jnp.where(mp == 0, own_rows(grad_encoded).astype(F32), 0.0)
+        + rms_back(feat_local.astype(F32), grad_normed)
     ).astype(BF)
     grad_codes = grad_feat.reshape(local, codes, pixels).transpose(0, 2, 1).reshape(-1, codes)
-    grad_proj = jnp.sum(lax.all_gather(t_dot(flat, grad_codes), "tile"), axis=0)
-    proj_rows = bands // (T * S)
-    grad_proj = lax.dynamic_slice_in_dim(grad_proj, (tile * S + seg) * proj_rows, proj_rows, 0)
+    grad_proj = project_sum(t_dot(flat, grad_codes).reshape(T * S, -1, codes))
     return (grad_proj, grad_in, grad_out)
 
 

time: 351 us -> 185 us (0.53)
  waiting for transfers between devices: 195 us -> 0 us
  Pallas kernels: 0 us -> 93 us
  blocking collectives: 65.8 us -> 0 us
  between operations: 15.2 us -> 1.73 us
  local copies, waits for them, and re-layouts: 15.7 us -> 28.2 us
    psum x4 -> x0, waiting for transfers between devices: 133 us -> none  [the longest x1 86.1 us: body(): lax.psum(grad_tok.reshape(rows, student).astype(BF), ('tile', 'segment',...]
    pallas_call x0 -> x5, Pallas kernels: none -> 93 us  [vmem_call(): pl.pallas_call(kernel, out_shape=outs, in_specs=[pl.BlockSpec(memory_spac...]
    all_gather x5 -> x0, blocking collectives: 65.8 us -> none  [the longest x1 15.8 us: body(): lax.all_gather(grad_own, 'tile')]
    reduce_scatter x2 -> x0, waiting for transfers between devices: 45 us -> none  [the longest x1 28 us: body(): lax.psum_scatter(partial.reshape(S * M, T, share * codes, -1), ('segment'...]
    all_gather x1 -> x0, waiting for transfers between devices: 17.2 us -> none  [body(): lax.all_gather(lax.all_gather(grad_own, 'tile'), ('segment', 'mp'))]
    transpose x0 -> x2, local copies, waits for them, and re-layouts: none -> 3.72 us  [the longest x1 2.27 us: body(): head_full = heads.transpose(1, 0, 2).reshape(dt, -1)]
    unnamed x30 -> x35, local copies, waits for them, and re-layouts: 1.22 us -> 4.78 us
  transfers between devices with their start and end apart: 7 -> 0, of which waited for: 6 -> 0; matrix products, arithmetic and copies ran while one was open for 5% -> 0% of each run, Pallas kernels for 0% -> 0%
where the time goes in v2:
time: 185 us; the launch traced here: 184 us
  Pallas kernels  93 us (50%)
  matrix products  47.7 us (26%)
  local copies, waits for them, and re-layouts  28.2 us (15%)
  other arithmetic  13.4 us (7%)
    pallas_call x5, Pallas kernels, vmem_call(): pl.pallas_call(kernel, out_shape=outs, in_specs=[pl.BlockSpec(memory_spac...  93 us
    dot_general x7, matrix products, dot(): return jnp.dot(a, b, preferred_element_type=F32)  22.9 us
    dot_general x7, matrix products, dot_t(): lax.dot_general(a, b, (((1,), (1,)), ((), ())), preferred_element_type=F32)  20.9 us
    convert_element_type x1, other arithmetic, body(): hid_act.astype(BF)  6.97 us
    unnamed x35, local copies, waits for them, and re-layouts  4.78 us
    dot_general x3, matrix products, t_dot(): lax.dot_general(a, b, (((0,), (0,)), ((), ())), preferred_element_type=F32)  3.95 us

profile of v2, /device:TPU:0, one launch (start us, length us, event | category | flops | bytes accessed | tf_op | source)
XLA Modules:
  0.0 184.1 jit_solution(8406799133342257306)
XLA Ops:
  0.6 1.4 convolution_convert_fusion.5
  4.0 10.4 %gather_tile.1 = (bf16[4,16,768]{2,1,0:T(8,128)(2,1)}, bf16[4,4,2048]{2,1,0:T(4,128)(2,1)}) custom-call(bf16[16,768]{1,0:T(8,128)(2,1)} %reshape.241.feat_ref, bf16[4,2048]{1,0:T(4,128)(2,1)} %band_ref.1), custom_call_target="tpu_custom_call" | custom-call | tf_op jit(solution)/shard_map/gather_tile/pallas_call | solution.py:79
  15.3 2.1 %convolution_convert_fusion = bf16[64,2048]{1,0:T(8,128)(2,1)S(1)} fusion(bf16[512,4096]{1,0:T(8,128)(2,1)} %param.17, s32[]{:T(128)S(6)} %select_n.51, s32[]{:T(128)S(6)} %select_n.50, bf16[48,2048]{1,0:T(8,128)(2,1)} %param.15, bf16[16,2048]{1,0:T(8,128)(2,1)S(1)} %reshape.242), kind=kOutput, calls=%fused_computation.16 | convolution fusion | flops 134479872 | bytes 2621448 | tf_op jit(solution)/shard_map/dot_general | solution.py:35
  19.9 2.2 %fusion.47 = f32[64,1536]{1,0:T(8,128)S(1)} fusion(bf16[64,768]{1,0:T(8,128)(2,1)S(1)} %multiply_convert_fusion.6, bf16[768,1536]{1,0:T(8,128)(2,1)} %param.13), kind=kOutput, calls=%fused_computation.86 | convolution fusion | flops 150994944 | bytes 2850816 | tf_op jit(solution)/shard_map/dot_general | solution.py:35
  22.9 1.2 convolution_convert_fusion.4.part_ref
  25.0 16.6 %fold_exchange.1 = (bf16[4,64,512]{2,1,0:T(8,128)(2,1)}, bf16[2,64,768]{2,1,0:T(8,128)(2,1)}, bf16[2,512,336]{2,1,0:T(8,128)(2,1)}) custom-call(bf16[4,64,512]{2,1,0:T(8,128)(2,1)} %bitcast.102, bf16[64,768]{1,0:T(8,128)(2,1)} %convolution_convert_fusion.4.part_ref, bf16[512,336]{1,0:T(8,128)(2,1)} %copy.58.head_ref), custom_call_target="tpu_custom_call" | custom-call | tf_op jit(solution)/shard_map/fold_exchange/pallas_call | solution.py:79
  41.6 2.3 %copy.61 = bf16[512,2,336]{0,2,1:T(8,128)(2,1)} copy(bf16[512,2,336]{2,0,1:T(8,128)(2,1)} %bitcast.106) | data formatting | bytes 1376256 | tf_op jit(solution)/shard_map/transpose | solution.py:340
  45.2 1.7 slice_bitcast_fusion
  48.0 4.5 %convolution_add_fusion = f32[64,16,2048]{2,1,0:T(8,128)} fusion(bf16[64,16,48]{2,1,0:T(8,128)(2,1)S(1)} %convert_element_type.193, bf16[48,2048,1]{1,0,2:T(8,128)(2,1)S(1)} %reshape.265, f32[16,2048]{1,0:T(8,128)S(1)} %bitcast.109), kind=kOutput, calls=%fused_computation.9 | convolution fusion | flops 203423744 | bytes 8814592 | tf_op jit(solution)/shard_map/dot_general | solution.py:35
  52.8 1.1 reduce_sum.70
  53.9 4.3 %multiply_reduce_fusion.1 = (f32[64,16]{1,0:T(8,128)S(1)}, bf16[64,16,2048]{2,1,0:T(8,128)(2,1)}) fusion(f32[16,2048]{1,0:T(8,128)S(1)} %convert_element_type.189, bf16[48,2048]{1,0:T(8,128)(2,1)} %param.15, f32[64,16,48]{2,1,0:T(8,128)S(1)} %reshape.252, f32[64,16,48]{2,1,0:T(8,128)} %reduce_sum.70), kind=kOutput, calls=%fused_computation.7 | convolution fusion | flops 211909632 | bytes 4919296 | tf_op jit(solution)/shard_map/dot_general | solution.py:35
  58.3 7.0 %multiply_convert_fusion.1 = bf16[1024,2048]{1,0:T(8,128)(2,1)} fusion(f32[64,16,2048]{2,1,0:T(8,128)} %convolution_add_fusion, f32[1024]{0:T(1024)S(1)} %rsqrt.37), kind=kLoop, calls=%fused_computation.3 | loop fusion | flops 20971520 | bytes 12587008 | tf_op jit(solution)/shard_map/convert_element_type | solution.py:355
  65.3 7.3 %convolution_convert_fusion.1 = bf16[1024,672]{0,1:T(8,128)(2,1)} fusion(bf16[512,672]{0,1:T(8,128)(2,1)S(1)} %bitcast.108, bf16[1024,2048]{1,0:T(8,128)(2,1)} %multiply_convert_fusion.1, bf16[4096,512]{1,0:T(8,128)(2,1)} %param.18, s32[]{:T(128)S(6)} %select_n.51, bf16[1024,2048]{1,0:T(8,128)(2,1)} %bitcast.115, s32[]{:T(128)S(6)} %select_n.50, ...), kind=kOutput, calls=%fused_computation.22 | convolution fusion | flops 2854912000 | bytes 9404428 | tf_op jit(solution)/shard_map/dot_general | solution.py:35
  72.5 2.6 %copy.62 = bf16[1024,672]{1,0:T(8,128)(2,1)} copy(bf16[1024,672]{0,1:T(8,128)(2,1)} %convolution_convert_fusion.1) | data formatting | bytes 2752512 | tf_op jit(solution)/shard_map/convert_element_type | solution.py:356
  76.0 1.4 copy.64
  77.4 1.3 reshape_reshape.14.target_ref
  81.0 39.6 %rebuilt_exchange.1 = bf16[2,2,2,4,32,672]{5,4,3,2,1,0:T(8,128)(2,1)} custom-call(bf16[2,2,2,4,32,672]{5,4,3,2,1,0:T(8,128)(2,1)} %bitcast.96, bf16[2,32,672]{2,1,0:T(8,128)(2,1)} %reshape_reshape.14.target_ref, f32[2,32,672]{2,1,0:T(8,128)} %compare_select_fusion.factor_ref), custom_call_target="tpu_custom_call" | custom-call | tf_op jit(solution)/shard_map/rebuilt_exchange/pallas_call | solution.py:79
  120.7 2.7 %convolution_convert_fusion.2 = bf16[1024,512]{1,0:T(8,128)(2,1)S(1)} fusion(bf16[1024,672]{1,0:T(8,128)(2,1)} %bitcast.101, bf16[512,672]{0,1:T(8,128)(2,1)} %bitcast.107), kind=kOutput, calls=%fused_computation.23 | convolution fusion | flops 705167360 | bytes 3112960 | tf_op jit(solution)/shard_map/dot_general | solution.py:39
  123.8 9.4 %multiply_reduce_fusion = (f32[1024]{0:T(1024)S(1)}, bf16[1024,2048]{1,0:T(8,128)(2,1)S(1)}) fusion(f32[64,16,2048]{2,1,0:T(8,128)} %convolution_add_fusion, f32[1024]{0:T(1024)S(1)} %rsqrt.37, bf16[1024,512]{1,0:T(8,128)(2,1)S(1)} %convolution_convert_fusion.2, bf16[4096,512]{1,0:T(8,128)(2,1)S(1)} %copy-done.14, s32[]{:T(128)S(6)} %select_n.51), kind=kOutput, calls=%fused_computation.1 | convolution fusion | flops 2191522816 | bytes 15736836 | tf_op jit(solution)/shard_map/dot_general | solution.py:39
  133.3 1.5 fusion.20
  134.8 2.0 %fusion.21 = bf16[1024,48]{0,1:T(8,128)(2,1)} fusion(f32[1024,48]{0,1:T(8,128)S(1)} %convolution_multiply_fusion.1, f32[1024,48]{0,1:T(8,128)S(1)} %fusion.20, bf16[48,2048]{1,0:T(8,128)(2,1)S(1)} %bitcast.105, bf16[1024,2048]{1,0:T(8,128)(2,1)S(1)} %get-tuple-element.32, f32[1024]{0:T(1024)S(1)} %rsqrt.37), kind=kOutput, calls=%fused_computation.29 | convolution fusion | flops 201523200 | bytes 4886528 | tf_op jit(solution)/shard_map/dot_general | solution.py:39
  136.8 1.1 copy.65
  138.8 18.1 %token_sum.1 = bf16[4,16,768]{2,1,0:T(8,128)(2,1)} custom-call(bf16[4,16,768]{2,1,0:T(8,128)(2,1)} %convert_element_type.208.part_ref), custom_call_target="tpu_custom_call" | custom-call | tf_op jit(solution)/shard_map/token_sum/pallas_call | solution.py:79
  157.0 1.7 fusion.4
  158.7 3.1 %convolution_convert_fusion.3 = bf16[64,768]{1,0:T(8,128)(2,1)} fusion(bf16[64,1536]{1,0:T(8,128)(2,1)S(1)} %fusion.4, bf16[768,1536]{1,0:T(8,128)(2,1)} %param.13), kind=kOutput, calls=%fused_computation.30 | convolution fusion | flops 151044096 | bytes 2654208 | tf_op jit(solution)/shard_map/dot_general | solution.py:39
  161.9 1.6 reshape.249
  163.4 1.6 reshape_reshape.15
  168.4 1.1 fusion.27
  170.7 8.2 %project_sum.1 = f32[28,16]{1,0:T(8,128)} custom-call(f32[8,28,16]{2,1,0:T(8,128)} %copy.69.part_ref), custom_call_target="tpu_custom_call" | custom-call | tf_op jit(solution)/shard_map/project_sum/pallas_call | solution.py:79
  178.9 1.4 copy.70
  180.3 1.9 %fusion.33 = f32[96,1536]{1,0:T(8,128)} fusion(bf16[64,1536]{1,0:T(8,128)(2,1)S(1)} %fusion.4, bf16[64,768]{1,0:T(8,128)(2,1)} %copy-done.8, s32[]{:T(128)S(6)} %select_n.60), kind=kOutput, calls=%fused_computation.61 | convolution fusion | flops 18874368 | bytes 802820 | tf_op jit(solution)/shard_map/dot_general | solution.py:43
  182.2 1.9 %fusion.31 = f32[1536,96]{0,1:T(8,128)} fusion(bf16[64,768]{1,0:T(8,128)(2,1)} %bitcast.111, s32[]{:T(128)S(6)} %select_n.60, f32[64,1536]{1,0:T(8,128)S(1)} %copy-done.3), kind=kOutput, calls=%fused_computation.59 | convolution fusion | flops 19759104 | bytes 999428 | tf_op jit(solution)/shard_map/dot_general | solution.py:43
  (85 shorter events, 18.2 us)
Async XLA Ops:
  0.6 22.2 %copy-start = (bf16[1536,768]{1,0:T(8,128)(2,1)S(1)}, bf16[1536,768]{1,0:T(8,128)(2,1)}, u32[]{:S(2)}) copy-start(bf16[1536,768]{1,0:T(8,128)(2,1)} %param.14) | copy-start | bytes 7077892
  2.2 16.0 %copy-start.4 = (bf16[16,48,16]{1,0,2:T(8,128)(2,1)}, bf16[16,48,16]{1,0,2:T(8,128)(2,1)S(1)}, u32[]{:S(2)}) copy-start(bf16[16,48,16]{1,0,2:T(8,128)(2,1)S(1)} %reshape.240) | copy-start | bytes 73732
  14.4 4.9 %copy-start.9 = (bf16[4,16,768]{2,1,0:T(8,128)(2,1)S(1)}, bf16[4,16,768]{2,1,0:T(8,128)(2,1)}, u32[]{:S(2)}) copy-start(bf16[4,16,768]{2,1,0:T(8,128)(2,1)} %get-tuple-element.8) | copy-start | bytes 294916
  17.4 6.6 %copy-start.10 = (bf16[512,336]{0,1:T(8,128)(2,1)S(1)}, bf16[512,336]{0,1:T(8,128)(2,1)}, u32[]{:S(2)}) copy-start(bf16[512,336]{0,1:T(8,128)(2,1)} %param.19) | copy-start | bytes 1032196
  19.9 24.0 %copy-start.8 = (bf16[64,768]{1,0:T(8,128)(2,1)}, bf16[64,768]{1,0:T(8,128)(2,1)S(1)}, u32[]{:S(2)}) copy-start(bf16[64,768]{1,0:T(8,128)(2,1)S(1)} %multiply_convert_fusion.6) | copy-start | bytes 294916
  22.1 0.8 copy-start.2
  58.3 7.0 %copy-start.7 = (bf16[512,2,336]{0,2,1:T(8,128)(2,1)S(1)}, bf16[512,2,336]{0,2,1:T(8,128)(2,1)}, u32[]{:S(2)}) copy-start(bf16[512,2,336]{0,2,1:T(8,128)(2,1)} %copy.61) | copy-start | bytes 2064388
  65.3 9.8 %copy-start.1 = (bf16[2,8,48,224]{3,2,1,0:T(8,128)(2,1)S(1)}, bf16[2,8,48,224]{3,2,1,0:T(8,128)(2,1)}, u32[]{:S(2)}) copy-start(bf16[2,8,48,224]{3,2,1,0:T(8,128)(2,1)} %param.10) | copy-start | bytes 1032196
  72.5 6.2 %copy-start.13 = (s32[2,32]{1,0:T(2,128)S(1)}, s32[2,32]{1,0:T(2,128)}, u32[]{:S(2)}) copy-start(s32[2,32]{1,0:T(2,128)} %param.11) | copy-start | bytes 772
  120.6 2.7 %copy-start.11 = (bf16[48,2048]{1,0:T(8,128)(2,1)S(1)}, bf16[48,2048]{1,0:T(8,128)(2,1)}, u32[]{:S(2)}) copy-start(bf16[48,2048]{1,0:T(8,128)(2,1)} %param.15) | copy-start | bytes 589828
  120.7 3.2 %copy-start.14 = (bf16[4096,512]{1,0:T(8,128)(2,1)S(1)}, bf16[4096,512]{1,0:T(8,128)(2,1)}, u32[]{:S(2)}) copy-start(bf16[4096,512]{1,0:T(8,128)(2,1)} %param.18) | copy-start | bytes 12582916
  123.8 9.5 %copy-start.15 = (bf16[64,16,2048]{2,1,0:T(8,128)(2,1)S(1)}, bf16[64,16,2048]{2,1,0:T(8,128)(2,1)}, u32[]{:S(2)}) copy-start(bf16[64,16,2048]{2,1,0:T(8,128)(2,1)} %get-tuple-element.30) | copy-start | bytes 12582916
  133.3 1.5 copy-start.6
  134.8 22.2 %copy-start.3 = (f32[64,1536]{1,0:T(8,128)S(1)}, f32[64,1536]{1,0:T(8,128)}, u32[]{:S(2)}) copy-start(f32[64,1536]{1,0:T(8,128)} %copy-done.2) | copy-start | bytes 1179652
  136.8 28.2 %copy-start.12 = (f32[8,1,2,768]{3,2,0,1:T(2,128)S(1)}, f32[8,1,2,768]{3,2,0,1:T(2,128)}, u32[]{:S(2)}) copy-start(f32[8,1,2,768]{3,2,0,1:T(2,128)} %reshape.258) | copy-start | bytes 147460
  136.8 31.5 %copy-start.5 = (bf16[16,48,16]{1,0,2:T(8,128)(2,1)S(1)}, bf16[16,48,16]{1,0,2:T(8,128)(2,1)}, u32[]{:S(2)}) copy-start(bf16[16,48,16]{1,0,2:T(8,128)(2,1)} %copy-done.4) | copy-start | bytes 73732

commit v3 on v2

--- a/solution.py
+++ b/solution.py
@@ -146,14 +146,88 @@
     return vmem_call(kernel, "fold_exchange", 1, outs, scratch, fold, part, head)
 
 
-def rebuilt_exchange(part, target, factor):
-    C, S, M, T, q, R = part.shape
+def teacher(x64, embed, folded, d_out, headt, target, factor, pixels):
+    S, M, T = (lax.axis_size(a) for a in ("segment", "mp", "tile"))
+    C, q, R = target.shape
+    owners = S * M * T
+    group = min(owners, 256 // q)
+    rows = group * q
+    blocks = owners // group
+    K = x64.shape[1]
+    dim = embed.shape[1]
+    dt = d_out.shape[1]
+    slabs, _, slab = folded.shape
+    hid = slabs * slab
+    step_cols = min(512, dim)
     most = max(S, M, T) - 1
 
-    def kernel(part_ref, target_ref, factor_ref, grad_ref, s_in, s_sum, m_in, m_sum, t_in, send, recv):
+    def kernel(
+        x_ref, embed_ref, fold_ref, dout_hbm, head_ref, target_ref, factor_ref, out_ref,
+        dout, pre_ref, slope_ref, scale_ref, unit_ref,
+        part_ref, grad_ref, s_in, s_sum, m_in, m_sum, t_in, send, recv, load,
+    ):
         s, m, t = (lax.axis_index(a) for a in ("segment", "mp", "tile"))
         segs, mps, tiles = ring("segment"), ring("mp"), ring("tile")
-        greet(segs + mps + tiles)
+        fetch = pltpu.make_async_copy(dout_hbm.at[pl.ds(s * hid, hid)], dout, load)
+        fetch.start()
+        once = jnp.logical_and(s == 0, m == 0).astype(F32)
+        own_cols = pl.ds(pl.multiple_of(t * dt, dt), dt)
+
+        def scales(c, i):
+            x = x_ref[c, pl.ds(i * rows, rows), :]
+            total = jnp.zeros((rows, 1), F32)
+            unit = jnp.zeros((rows, pixels), F32)
+            for b in range(dim // step_cols):
+                cols = slice(b * step_cols, (b + 1) * step_cols)
+                e = dot(x, embed_ref[:, cols]).astype(BF)
+                e32 = e.astype(F32)
+                total = total + jnp.sum(e32 * e32, axis=1, keepdims=True)
+                unit = unit + dot_t(e, embed_ref[:pixels, cols])
+            scale = lax.rsqrt(total / dim + 1e-05)
+            scale_ref[c, i] = scale
+            unit_ref[c, i] = unit * scale
+
+        def forward(c, i):
+            scales(c, i)
+            x = x_ref[c, pl.ds(i * rows, rows), :]
+            scale = scale_ref[c, i]
+
+            def hidden(h, acc):
+                pre = scale * dot(x, fold_ref[h])
+                act, slope = gelu_and_slope(pre)
+                pre_ref[c, i, h] = pre
+                slope_ref[c, i, h] = slope
+                return acc + dot(act.astype(BF), dout[pl.ds(pl.multiple_of(h * slab, slab), slab), :])
+
+            start = once * dot(x, embed_ref[:, own_cols]).astype(BF).astype(F32)
+            acc = lax.fori_loop(0, slabs, hidden, start)
+            part = dot_t(acc.astype(BF), head_ref[...]).astype(BF)
+            part_ref[c, pl.ds(i * group, group)] = part.reshape(group, q, R)
+
+        def backward(c, i):
+            grad = grad_ref[c, pl.ds(i * group, group)].reshape(rows, R)
+            gd = dot(grad, head_ref[...]).astype(BF)
+            direct = once * dot_t(gd, embed_ref[:pixels, own_cols])
+
+            def hidden(h, carry):
+                acc, along = carry
+                back = dot_t(gd, dout[pl.ds(pl.multiple_of(h * slab, slab), slab), :])
+                gh = slope_ref[c, i, h] * back
+                along = along + jnp.sum(gh * pre_ref[c, i, h], axis=1, keepdims=True)
+                return acc + dot_t(gh.astype(BF), fold_ref[h, :pixels, :]), along
+
+            acc, along = lax.fori_loop(
+                0, slabs, hidden, (jnp.zeros((rows, pixels), F32), jnp.zeros((rows, 1), F32))
+            )
+            result = scale_ref[c, i] * (acc - unit_ref[c, i] * (along / dim)) + direct
+            out_ref[c, pl.ds(i * rows, rows), :] = result.astype(BF)
+
+        def over(function, c):
+            if blocks == 1:
+                function(c, 0)
+            else:
+                lax.fori_loop(0, blocks, lambda i, _: (function(c, i), 0)[1], 0)
+
         live = [None] * C
         everything = []
 
@@ -168,16 +242,15 @@
             if stage > 0:
                 finish(live[c])
             if stage == 0:
-                launch(c, 0, segs, lambda k, p: part_ref.at[c, p["segment"]], lambda k: s_in.at[c, k])
+                launch(c, 0, segs, lambda k, p: part_ref.at[c, pl.ds(p["segment"] * M * T, M * T)], lambda k: s_in.at[c, k])
             if stage == 1:
-                for other in range(M):
-                    total = part_ref[c, s, other].astype(F32)
-                    for k in range(S - 1):
-                        total = total + s_in[c, k, other].astype(F32)
-                    s_sum[c, other] = total.astype(BF)
-                launch(c, 1, mps, lambda k, p: s_sum.at[c, p["mp"]], lambda k: m_in.at[c, k])
+                total = part_ref[c, pl.ds(s * M * T, M * T)].astype(F32)
+                for k in range(S - 1):
+                    total = total + s_in[c, k].astype(F32)
+                s_sum[c] = total.astype(BF)
+                launch(c, 1, mps, lambda k, p: s_sum.at[c, pl.ds(p["mp"] * T, T)], lambda k: m_in.at[c, k])
             if stage == 2:
-                total = s_sum[c, m].astype(F32)
+                total = s_sum[c, pl.ds(m * T, T)].astype(F32)
                 for k in range(M - 1):
                     total = total + m_in[c, k].astype(F32)
                 m_sum[c] = total.astype(BF)
@@ -187,35 +260,62 @@
                 for k in range(T - 1):
                     total = total + t_in[c, k].astype(F32)
                 grad = factor_ref[c] * (total - target_ref[c].astype(F32))
-                grad_ref[c, s, m, t] = grad.astype(BF)
-                own = grad_ref.at[c, s, m, t]
+                place = (s * M + m) * T + t
+                grad_ref[c, place] = grad.astype(BF)
+                own = grad_ref.at[c, place]
                 launch(c, 3, tiles, lambda k, p: own, lambda k: own)
             if stage == 4:
-                own = grad_ref.at[c, s, m]
+                own = grad_ref.at[c, pl.ds((s * M + m) * T, T)]
                 launch(c, 4, mps, lambda k, p: own, lambda k: own)
             if stage == 5:
-                own = grad_ref.at[c, s]
+                own = grad_ref.at[c, pl.ds(s * M * T, M * T)]
                 launch(c, 5, segs, lambda k, p: own, lambda k: own)
 
-        for step in range(7 + C - 1):
+        greet(segs + mps + tiles)
+        fetch.wait()
+        for step in range(7 + C):
             for c in range(C):
-                if 0 <= step - c <= 6:
-                    advance(c, step - c)
+                stage = step - c - 1
+                if 0 <= stage <= 6:
+                    advance(c, stage)
+            for c in range(C):
+                if step == c:
+                    over(forward, c)
+                if step - c - 1 == 6:
+                    over(backward, c)
         for copy in everything:
             copy.wait_send()
 
+    vm = pltpu.VMEM
     scratch = [
-        pltpu.VMEM((C, S - 1, M, T, q, R), BF),
-        pltpu.VMEM((C, M, T, q, R), BF),
-        pltpu.VMEM((C, M - 1, T, q, R), BF),
-        pltpu.VMEM((C, T, q, R), BF),
-        pltpu.VMEM((C, T - 1, q, R), BF),
+        vm((hid, dt), BF),
+        vm((C, blocks, slabs, rows, slab), F32),
+        vm((C, blocks, slabs, rows, slab), F32),
+        vm((C, blocks, rows, 1), F32),
+        vm((C, blocks, rows, pixels), F32),
+        vm((C, owners, q, R), BF),
+        vm((C, owners, q, R), BF),
+        vm((C, S - 1, M * T, q, R), BF),
+        vm((C, M * T, q, R), BF),
+        vm((C, M - 1, T, q, R), BF),
+        vm((C, T, q, R), BF),
+        vm((C, T - 1, q, R), BF),
         DMA((6, C, most)),
         DMA((6, C, most)),
+        DMA,
     ]
-    return vmem_call(
-        kernel, "rebuilt_exchange", 2, jax.ShapeDtypeStruct(part.shape, BF), scratch, part, target, factor
-    )
+    whole = pl.BlockSpec(memory_space=pltpu.VMEM)
+    return pl.pallas_call(
+        kernel,
+        out_shape=jax.ShapeDtypeStruct((C, owners * q, pixels), BF),
+        in_specs=[whole] * 3 + [pl.BlockSpec(memory_space=pl.ANY)] + [whole] * 3,
+        out_specs=whole,
+        scratch_shapes=scratch,
+        compiler_params=pltpu.CompilerParams(
+            collective_id=2, has_side_effects=True, vmem_limit_bytes=56 << 20
+        ),
+        name="teacher",
+    )(x64.reshape(C, owners * q, K), embed, folded, d_out, headt, target, factor)
 
 
 def token_sum(part):
@@ -311,7 +411,6 @@
     dim = tok_embed.shape[1]
     dt = dec_in.shape[0]
     hid = dec_in.shape[1] // S
-    once = jnp.logical_and(seg == 0, mp == 0).astype(F32)
 
     patches = spectra.reshape(local, pixels, bands)
     flat = patches.reshape(local * pixels, bands)
@@ -327,33 +426,23 @@
     embed = jnp.concatenate([tok_embed, band_all], axis=0)
     embed_z = lax.dynamic_slice_in_dim(embed, tile * dt, dt, 1)
     d_in = lax.dynamic_slice_in_dim(dec_in, seg * hid, hid, 1)
-    d_out = lax.dynamic_slice_in_dim(dec_out, seg * hid, hid, 0)
     fold_part = dot(embed_z, d_in).astype(BF).reshape(-1, T, hid // T).transpose(1, 0, 2)
 
     feats32 = feats.astype(F32)
     normed = (feats32 * inv_rms(feats32)).astype(BF)
     pre_act, pre_slope = gelu_and_slope(dot(normed, enc_in))
     act_out = pre_act.astype(BF)
-    folded, summed, heads = fold_exchange(fold_part, dot(act_out, enc_out).astype(BF), head)
-    folded = folded.transpose(1, 0, 2).reshape(-1, hid)
-    fold_tok, fold_band = folded[:pixels], folded[pixels:]
-    head_full = heads.transpose(1, 0, 2).reshape(dt, -1)
+    folded, summed, heads = fold_exchange(fold_part, dot(act_out, enc_out).astype(BF), head.T)
+    headt = heads.reshape(-1, dt)
+    if hid // T < 128:
+        folded = folded.transpose(1, 0, 2).reshape(1, -1, hid)
     summed = jnp.sum(summed.astype(F32), axis=0)
     encoded = (feats32 + summed).astype(BF)
 
     tokens = rows * codes
     tok = encoded.reshape(tokens, pixels)
-    embedded = (
-        dot(tok, tok_embed).reshape(rows, codes, dim) + band_all.astype(F32)
-    ).reshape(tokens, dim).astype(BF)
-    scaling = inv_rms(embedded.astype(F32))
-    hid_pre = scaling * (
-        dot(tok, fold_tok).reshape(rows, codes, hid) + fold_band.astype(F32)
-    ).reshape(tokens, hid)
-    hid_act, hid_slope = gelu_and_slope(hid_pre)
-    embedded_z = lax.dynamic_slice_in_dim(embedded, tile * dt, dt, 1)
-    decoded = (once * embedded_z.astype(F32) + dot(hid_act.astype(BF), d_out)).astype(BF)
-    partial = dot(decoded, head_full).astype(BF)
+    which = jnp.broadcast_to(jnp.eye(codes, dtype=BF), (rows, codes, codes)).reshape(tokens, codes)
+    x64 = jnp.concatenate([tok, which], axis=1)
     place = (seg * M + mp) * piece
 
     def mine(a):
@@ -372,20 +461,17 @@
     column = jnp.arange(pixels * width, dtype=jnp.int32) // width
     mask = (column[None, :] < jnp.repeat(own_valid, codes)[:, None]).astype(F32)
     block = (parts, piece * codes, pixels * width)
-    grad_rebuilt = rebuilt_exchange(
-        partial.reshape(parts, S, M, T, piece * codes, -1),
+    grad_tok = teacher(
+        x64,
+        embed,
+        folded,
+        dec_out,
+        headt,
         target.reshape(block),
         (loss_scale * mask).reshape(block),
-    ).reshape(tokens, -1)
-
-    grad_decoded = dot_t(grad_rebuilt, head_full).astype(BF)
-    grad_hid = hid_slope * dot_t(grad_decoded, d_out)
-    tok_z = lax.dynamic_slice_in_dim(tok_embed, tile * dt, dt, 1)
-    unit_tok = dot_t((embedded.astype(F32) * scaling).astype(BF), tok_embed)
-    along = jnp.sum(grad_hid * hid_pre, axis=1, keepdims=True) / dim
-    grad_tok = scaling * (dot_t(grad_hid.astype(BF), fold_tok) - unit_tok * along)
-    grad_tok = grad_tok + once * dot_t(grad_decoded, tok_z)
-    grad_encoded = token_sum(grad_tok.reshape(T, local, student).astype(BF)).reshape(rows, student)
+        pixels,
+    )
+    grad_encoded = token_sum(grad_tok.reshape(T, local, student)).reshape(rows, student)
 
     grad_act = (pre_slope * dot_t(grad_encoded, enc_out)).astype(BF)
     columns = student // (T * S)

time: 185 us -> 150 us (0.81)
  matrix products: 47.7 us -> 13.5 us
  Pallas kernels: 93 us -> 114 us
  local copies, waits for them, and re-layouts: 28.2 us -> 15.1 us
  other arithmetic: 13.4 us -> 4.66 us
    pallas_call x0 -> x1, Pallas kernels: none -> 59.9 us  [teacher(): pl.pallas_call(kernel, out_shape=jax.ShapeDtypeStruct((C, owners * q, pix...]
    pallas_call x5 -> x4, Pallas kernels: 93 us -> 54.2 us  [vmem_call(): pl.pallas_call(kernel, out_shape=outs, in_specs=[pl.BlockSpec(memory_spac...]
    dot_general x7 -> x2, matrix products: 20.9 us -> 2.7 us  [dot_t(): lax.dot_general(a, b, (((1,), (1,)), ((), ())), preferred_element_type=F32)]
    dot_general x7 -> x4, matrix products: 22.9 us -> 6.84 us  [dot(): return jnp.dot(a, b, preferred_element_type=F32)]
    convert_element_type x2 -> x1, other arithmetic: 6.99 us -> 0.01 us  [body(): jnp.eye(codes, dtype=BF)]
    convert_element_type x5 -> x0, local copies, waits for them, and re-layouts: 4.9 us -> none  [the longest x1 2.59 us: body(): partial = dot(decoded, head_full).astype(BF)]
    transpose x1 -> x0, local copies, waits for them, and re-layouts: 2.27 us -> none  [body(): head_full = heads.transpose(1, 0, 2).reshape(dt, -1)]
    reshape x0 -> x1, local copies, waits for them, and re-layouts: none -> 1.87 us  [body(): grad_tok.reshape(T, local, student)]
where the time goes in v3:
time: 150 us; the launch traced here: 149 us
  Pallas kernels  114 us (76%)
  local copies, waits for them, and re-layouts  15.1 us (10%)
  matrix products  13.5 us (9%)
  other arithmetic  4.66 us (3%)
  between operations  1.67 us (1%)
    pallas_call x1, Pallas kernels, teacher(): pl.pallas_call(kernel, out_shape=jax.ShapeDtypeStruct((C, owners * q, pix...  59.9 us
    pallas_call x4, Pallas kernels, vmem_call(): pl.pallas_call(kernel, out_shape=outs, in_specs=[pl.BlockSpec(memory_spac...  54.2 us
    dot_general x4, matrix products, dot(): return jnp.dot(a, b, preferred_element_type=F32)  6.84 us
    dot_general x3, matrix products, t_dot(): lax.dot_general(a, b, (((0,), (0,)), ((), ())), preferred_element_type=F32)  4.01 us
    unnamed x26, local copies, waits for them, and re-layouts  3.82 us

profile of v3, /device:TPU:0, one launch (start us, length us, event | category | flops | bytes accessed | tf_op | source)
XLA Modules:
  0.0 149.2 jit_solution(2947787854635601859)
XLA Ops:
  0.7 1.4 convolution_convert_fusion.3
  2.2 0.7 fusion.15
  2.9 0.7 reshape.180.feat_ref
  3.6 10.4 %gather_tile.1 = (bf16[4,16,768]{2,1,0:T(8,128)(2,1)}, bf16[4,4,2048]{2,1,0:T(4,128)(2,1)}) custom-call(bf16[16,768]{1,0:T(8,128)(2,1)} %reshape.180.feat_ref, bf16[4,2048]{1,0:T(4,128)(2,1)} %band_ref.1), custom_call_target="tpu_custom_call" | custom-call | tf_op jit(solution)/shard_map/gather_tile/pallas_call | solution.py:79
  14.0 0.9 reshape.181
  14.9 0.9 constant_dynamic-update-slice_fusion.1
  15.8 0.7 copy-done.6
  16.5 2.1 %convolution_convert_fusion = bf16[64,2048]{1,0:T(8,128)(2,1)S(1)} fusion(bf16[512,4096]{1,0:T(8,128)(2,1)} %param.17, s32[]{:T(128)S(6)} %select_n.48, bf16[64,2048]{1,0:T(8,128)(2,1)S(1)} %constant_dynamic-update-slice_fusion.embed_ref, s32[]{:T(128)S(6)} %select_n.47), kind=kOutput, calls=%fused_computation.2 | convolution fusion | flops 134348800 | bytes 2424840 | tf_op jit(solution)/shard_map/dot_general | solution.py:35
  18.6 0.7 copy.62
  20.2 2.2 %fusion.16 = f32[64,1536]{1,0:T(8,128)S(1)} fusion(bf16[64,768]{1,0:T(8,128)(2,1)S(1)} %multiply_convert_fusion.1, bf16[768,1536]{1,0:T(8,128)(2,1)} %param.13), kind=kOutput, calls=%fused_computation.52 | convolution fusion | flops 150994944 | bytes 2850816 | tf_op jit(solution)/shard_map/dot_general | solution.py:35
  22.4 0.7 copy-done.4
  23.2 1.2 convolution_convert_fusion.2.part_ref
  24.3 16.6 %fold_exchange.1 = (bf16[4,64,512]{2,1,0:T(8,128)(2,1)}, bf16[2,64,768]{2,1,0:T(8,128)(2,1)}, bf16[2,336,512]{2,1,0:T(8,128)(2,1)}) custom-call(bf16[4,64,512]{2,1,0:T(8,128)(2,1)} %bitcast.69, bf16[64,768]{1,0:T(8,128)(2,1)} %convolution_convert_fusion.2.part_ref, bf16[336,512]{1,0:T(8,128)(2,1)} %bitcast.74), custom_call_target="tpu_custom_call" | custom-call | tf_op jit(solution)/shard_map/fold_exchange/pallas_call | solution.py:79
  40.9 1.0 convert_reduce_fusion
  41.9 0.3 reduce_sum.52
  42.2 1.3 reshape.189
  43.6 0.9 pad_maximum_fusion.x_ref
  44.7 0.6 convert_reduce_fusion.1
  45.9 0.7 compare_select_fusion.factor_ref
  46.7 0.9 constant_dynamic-slice_fusion.1
  47.8 0.5 copy.44
  48.3 1.3 reshape_reshape.14.target_ref
  49.6 59.9 %teacher.1 = bf16[2,512,48]{2,1,0:T(8,128)(2,1)} custom-call(bf16[2,512,64]{2,1,0:T(8,128)(2,1)} %pad_maximum_fusion.x_ref, bf16[64,2048]{1,0:T(8,128)(2,1)} %copy-done.6, bf16[4,64,512]{2,1,0:T(8,128)(2,1)} %get-tuple-element.11.fold_ref, bf16[4096,512]{1,0:T(8,128)(2,1)} %dout_hbm.1, bf16[672,512]{1,0:T(8,128)(2,1)} %bitcast.71, ...), custom_call_target="tpu_custom_call" | custom-call | tf_op jit(solution)/shard_map/teacher/pallas_call | solution.py:308
  109.5 1.9 %reshape.184.part_ref = bf16[4,16,768]{2,1,0:T(8,128)(2,1)} reshape(bf16[2,512,48]{2,1,0:T(8,128)(2,1)} %teacher.1) | data formatting | bytes 196608 | tf_op jit(solution)/shard_map/reshape | solution.py:474
  111.4 19.1 %token_sum.1 = bf16[4,16,768]{2,1,0:T(8,128)(2,1)} custom-call(bf16[4,16,768]{2,1,0:T(8,128)(2,1)} %reshape.184.part_ref), custom_call_target="tpu_custom_call" | custom-call | tf_op jit(solution)/shard_map/token_sum/pallas_call | solution.py:79
  130.5 1.9 %fusion.4 = f32[1536,96]{0,1:T(8,128)} fusion(bf16[64,768]{1,0:T(8,128)(2,1)} %bitcast.72, s32[]{:T(128)S(6)} %select_n.57, f32[64,1536]{1,0:T(8,128)S(1)} %copy-done.5), kind=kOutput, calls=%fused_computation.27 | convolution fusion | flops 19759104 | bytes 999428 | tf_op jit(solution)/shard_map/dot_general | solution.py:43
  132.4 1.9 %fusion = bf16[64,1536]{1,0:T(8,128)(2,1)S(1)} fusion(bf16[64,768]{1,0:T(8,128)(2,1)} %bitcast.73, bf16[1536,768]{1,0:T(8,128)(2,1)S(1)} %copy-done, f32[64,1536]{1,0:T(8,128)S(1)} %copy-done.5), kind=kOutput, calls=%fused_computation.1 | convolution fusion | flops 152764416 | bytes 3047424 | tf_op jit(solution)/shard_map/dot_general | solution.py:39
  134.3 1.9 %fusion.6 = f32[96,1536]{1,0:T(8,128)} fusion(bf16[64,1536]{1,0:T(8,128)(2,1)S(1)} %fusion, bf16[64,768]{1,0:T(8,128)(2,1)} %copy-done.8, s32[]{:T(128)S(6)} %select_n.57), kind=kOutput, calls=%fused_computation.29 | convolution fusion | flops 18874368 | bytes 802820 | tf_op jit(solution)/shard_map/dot_general | solution.py:43
  136.3 0.8 convolution_convert_fusion.1
  138.8 0.8 copy.48.part_ref
  139.6 8.2 %project_sum.1 = f32[28,16]{1,0:T(8,128)} custom-call(f32[8,28,16]{2,1,0:T(8,128)} %copy.48.part_ref), custom_call_target="tpu_custom_call" | custom-call | tf_op jit(solution)/shard_map/project_sum/pallas_call | solution.py:79
  147.8 1.4 copy.49
  (58 shorter events, 3.1 us)
Async XLA Ops:
  0.6 22.5 %copy-start = (bf16[1536,768]{1,0:T(8,128)(2,1)S(1)}, bf16[1536,768]{1,0:T(8,128)(2,1)}, u32[]{:S(2)}) copy-start(bf16[1536,768]{1,0:T(8,128)(2,1)} %param.14) | copy-start | bytes 7077892
  13.9 5.4 %copy-start.10 = (bf16[4,16,768]{2,1,0:T(8,128)(2,1)S(1)}, bf16[4,16,768]{2,1,0:T(8,128)(2,1)}, u32[]{:S(2)}) copy-start(bf16[4,16,768]{2,1,0:T(8,128)(2,1)} %get-tuple-element.8) | copy-start | bytes 294916
  15.8 0.7 copy-start.6
  19.5 4.9 %copy-start.3 = (f32[4,2,2,2,2,768]{5,4,0,3,2,1:T(2,128)}, f32[4,2,2,2,2,768]{5,4,0,3,2,1:T(2,128)S(1)}, u32[]{:S(2)}) copy-start(f32[4,2,2,2,2,768]{5,4,0,3,2,1:T(2,128)S(1)} %copy.63) | copy-start | bytes 589828
  20.2 4.2 %copy-start.8 = (bf16[64,768]{1,0:T(8,128)(2,1)}, bf16[64,768]{1,0:T(8,128)(2,1)S(1)}, u32[]{:S(2)}) copy-start(bf16[64,768]{1,0:T(8,128)(2,1)S(1)} %multiply_convert_fusion.1) | copy-start | bytes 294916
  22.4 0.8 copy-start.4
  24.3 20.1 %copy-start.11 = (s32[2,32]{1,0:T(2,128)S(1)}, s32[2,32]{1,0:T(2,128)}, u32[]{:S(2)}) copy-start(s32[2,32]{1,0:T(2,128)} %param.11) | copy-start | bytes 772
  49.6 80.9 %copy-start.5 = (f32[64,1536]{1,0:T(8,128)S(1)}, f32[64,1536]{1,0:T(8,128)}, u32[]{:S(2)}) copy-start(f32[64,1536]{1,0:T(8,128)} %copy-done.4) | copy-start | bytes 1179652
  132.4 3.8 %copy-start.1 = (bf16[768,1536]{1,0:T(8,128)(2,1)S(1)}, bf16[768,1536]{1,0:T(8,128)(2,1)}, u32[]{:S(2)}) copy-start(bf16[768,1536]{1,0:T(8,128)(2,1)} %param.13) | copy-start | bytes 7077892
  134.3 2.8 %copy-start.9 = (bf16[4,16,768]{2,1,0:T(8,128)(2,1)S(1)}, bf16[4,16,768]{2,1,0:T(8,128)(2,1)}, u32[]{:S(2)}) copy-start(bf16[4,16,768]{2,1,0:T(8,128)(2,1)} %token_sum.1) | copy-start | bytes 294916
  134.3 2.9 %copy-start.7 = (f32[16,16,48]{2,1,0:T(8,128)S(1)}, f32[16,16,48]{2,1,0:T(8,128)}, u32[]{:S(2)}) copy-start(f32[16,16,48]{2,1,0:T(8,128)} %get-tuple-element.25) | copy-start | bytes 147460
  136.3 2.2 %copy-start.2 = (bf16[2,8,48,224]{3,2,1,0:T(8,128)(2,1)S(1)}, bf16[2,8,48,224]{3,2,1,0:T(8,128)(2,1)}, u32[]{:S(2)}) copy-start(bf16[2,8,48,224]{3,2,1,0:T(8,128)(2,1)} %param.10) | copy-start | bytes 1032196

commit v4 on v3

--- a/solution.py
+++ b/solution.py
@@ -321,12 +321,16 @@
 def token_sum(part):
     T, rows, width = part.shape
     S, M = lax.axis_size("segment"), lax.axis_size("mp")
-    most = max(S, M, T) - 1
-
-    def kernel(part_ref, sum_ref, s_in, s_sum, m_in, m_sum, t_in, send, recv):
+    holders = S * M
+    most = max(holders, T) - 1
+
+    def kernel(part_ref, sum_ref, t_in, t_sum, h_in, send, recv):
         t = lax.axis_index("tile")
-        segs, mps, tiles = ring("segment"), ring("mp"), ring("tile")
-        greet(segs + mps + tiles)
+        tiles = ring("tile")
+        others = [
+            {"segment": shifted("segment", k // M), "mp": shifted("mp", k % M)} for k in range(1, holders)
+        ]
+        greet(tiles + others)
         everything = []
 
         def launch(stage, peers, source, landing):
@@ -337,34 +341,27 @@
             everything.extend(copies)
             finish(copies)
 
-        launch(0, segs, lambda p: part_ref, lambda k: s_in.at[k])
-        total = part_ref[...].astype(F32)
-        for k in range(S - 1):
-            total = total + s_in[k].astype(F32)
-        s_sum[...] = total.astype(BF)
-        launch(1, mps, lambda p: s_sum, lambda k: m_in.at[k])
-        total = s_sum[...].astype(F32)
-        for k in range(M - 1):
-            total = total + m_in[k].astype(F32)
-        m_sum[...] = total.astype(BF)
-        launch(2, tiles, lambda p: m_sum.at[p["tile"]], lambda k: t_in.at[k])
-        total = m_sum[t].astype(F32)
+        launch(0, tiles, lambda p: part_ref.at[p["tile"]], lambda k: t_in.at[k])
+        total = part_ref[t].astype(F32)
         for k in range(T - 1):
             total = total + t_in[k].astype(F32)
+        t_sum[...] = total.astype(BF)
+        launch(1, others, lambda p: t_sum, lambda k: h_in.at[k])
+        total = t_sum[...].astype(F32)
+        for k in range(holders - 1):
+            total = total + h_in[k].astype(F32)
         sum_ref[t] = total.astype(BF)
         own = sum_ref.at[t]
-        launch(3, tiles, lambda p: own, lambda k: own)
+        launch(2, tiles, lambda p: own, lambda k: own)
         for copy in everything:
             copy.wait_send()
 
     scratch = [
-        pltpu.VMEM((S - 1,) + part.shape, BF),
-        pltpu.VMEM(part.shape, BF),
-        pltpu.VMEM((M - 1,) + part.shape, BF),
-        pltpu.VMEM(part.shape, BF),
         pltpu.VMEM((T - 1, rows, width), BF),
-        DMA((4, most)),
-        DMA((4, most)),
+        pltpu.VMEM((rows, width), BF),
+        pltpu.VMEM((holders - 1, rows, width), BF),
+        DMA((3, most)),
+        DMA((3, most)),
     ]
     return vmem_call(kernel, "token_sum", 3, jax.ShapeDtypeStruct(part.shape, BF), scratch, part)
 
@@ -375,6 +372,7 @@
 
     def kernel(part_ref, sum_ref, slots, send, recv):
         s, t = lax.axis_index("segment"), lax.axis_index("tile")
+        me = t * M + lax.axis_index("mp")
         peers = [
             {"tile": shifted("tile", k // M), "mp": shifted("mp", k % M)} for k in range(1, count)
         ]
@@ -382,17 +380,18 @@
         copies = []
         for k, peer in enumerate(peers):
             copies.append(
-                push(part_ref.at[peer["tile"] * S + s], slots.at[k], send.at[k], recv.at[k], peer)
+                push(part_ref.at[peer["tile"] * S + s], slots.at[me], send.at[k], recv.at[k], peer)
             )
+        slots[me] = part_ref[t * S + s]
         finish(copies)
-        total = part_ref[t * S + s]
-        for k in range(count - 1):
+        total = slots[0]
+        for k in range(1, count):
             total = total + slots[k]
         sum_ref[...] = total
         for copy in copies:
             copy.wait_send()
 
-    scratch = [pltpu.VMEM((count - 1,) + part.shape[1:], F32), DMA((count - 1,)), DMA((count - 1,))]
+    scratch = [pltpu.VMEM((count,) + part.shape[1:], F32), DMA((count - 1,)), DMA((count - 1,))]
     return vmem_call(kernel, "project_sum", 4, jax.ShapeDtypeStruct(part.shape[1:], F32), scratch, part)
 
 

time: 150 us -> 148 us (0.987)
    pallas_call x4, Pallas kernels: 54.2 us -> 52.6 us  [vmem_call(): pl.pallas_call(kernel, out_shape=outs, in_specs=[pl.BlockSpec(memory_spac...]
where the time goes in v4:
time: 148 us
  Pallas kernels  113 us (76%)
  local copies, waits for them, and re-layouts  15.1 us (10%)
  matrix products  13.6 us (9%)
  other arithmetic  4.66 us (3%)
  between operations  1.67 us (1%)
    pallas_call x1, Pallas kernels, teacher(): pl.pallas_call(kernel, out_shape=jax.ShapeDtypeStruct((C, owners * q, pix...  59.9 us
    pallas_call x4, Pallas kernels, vmem_call(): pl.pallas_call(kernel, out_shape=outs, in_specs=[pl.BlockSpec(memory_spac...  52.6 us
    dot_general x4, matrix products, dot(): return jnp.dot(a, b, preferred_element_type=F32)  6.84 us
    dot_general x3, matrix products, t_dot(): lax.dot_general(a, b, (((0,), (0,)), ((), ())), preferred_element_type=F32)  4.02 us
    unnamed x26, local copies, waits for them, and re-layouts  3.82 us

profile of v4, /device:TPU:0, one launch (start us, length us, event | category | flops | bytes accessed | tf_op | source)
XLA Modules:
  0.0 147.5 jit_solution(13272569442982086083)
XLA Ops:
  0.7 1.4 convolution_convert_fusion.3
  2.2 0.7 fusion.15
  2.9 0.7 reshape.180.feat_ref
  3.6 10.4 %gather_tile.1 = (bf16[4,16,768]{2,1,0:T(8,128)(2,1)}, bf16[4,4,2048]{2,1,0:T(4,128)(2,1)}) custom-call(bf16[16,768]{1,0:T(8,128)(2,1)} %reshape.180.feat_ref, bf16[4,2048]{1,0:T(4,128)(2,1)} %band_ref.1), custom_call_target="tpu_custom_call" | custom-call | tf_op jit(solution)/shard_map/gather_tile/pallas_call | solution.py:79
  14.0 0.9 reshape.181
  14.9 0.9 constant_dynamic-update-slice_fusion.1
  15.8 0.7 copy-done.6
  16.5 2.1 %convolution_convert_fusion = bf16[64,2048]{1,0:T(8,128)(2,1)S(1)} fusion(bf16[512,4096]{1,0:T(8,128)(2,1)} %param.17, s32[]{:T(128)S(6)} %select_n.48, bf16[64,2048]{1,0:T(8,128)(2,1)S(1)} %constant_dynamic-update-slice_fusion.embed_ref, s32[]{:T(128)S(6)} %select_n.47), kind=kOutput, calls=%fused_computation.2 | convolution fusion | flops 134348800 | bytes 2424840 | tf_op jit(solution)/shard_map/dot_general | solution.py:35
  18.6 0.7 copy.62
  20.2 2.2 %fusion.16 = f32[64,1536]{1,0:T(8,128)S(1)} fusion(bf16[64,768]{1,0:T(8,128)(2,1)S(1)} %multiply_convert_fusion.1, bf16[768,1536]{1,0:T(8,128)(2,1)} %param.13), kind=kOutput, calls=%fused_computation.52 | convolution fusion | flops 150994944 | bytes 2850816 | tf_op jit(solution)/shard_map/dot_general | solution.py:35
  22.4 0.7 copy-done.4
  23.2 1.2 convolution_convert_fusion.2.part_ref
  24.3 16.6 %fold_exchange.1 = (bf16[4,64,512]{2,1,0:T(8,128)(2,1)}, bf16[2,64,768]{2,1,0:T(8,128)(2,1)}, bf16[2,336,512]{2,1,0:T(8,128)(2,1)}) custom-call(bf16[4,64,512]{2,1,0:T(8,128)(2,1)} %bitcast.69, bf16[64,768]{1,0:T(8,128)(2,1)} %convolution_convert_fusion.2.part_ref, bf16[336,512]{1,0:T(8,128)(2,1)} %bitcast.74), custom_call_target="tpu_custom_call" | custom-call | tf_op jit(solution)/shard_map/fold_exchange/pallas_call | solution.py:79
  40.9 1.0 convert_reduce_fusion
  41.9 0.3 reduce_sum.52
  42.2 1.3 reshape.189
  43.6 0.9 pad_maximum_fusion.x_ref
  44.7 0.6 convert_reduce_fusion.1
  45.9 0.7 compare_select_fusion.factor_ref
  46.7 0.9 constant_dynamic-slice_fusion.1
  47.8 0.5 copy.44
  48.3 1.3 reshape_reshape.14.target_ref
  49.6 59.9 %teacher.1 = bf16[2,512,48]{2,1,0:T(8,128)(2,1)} custom-call(bf16[2,512,64]{2,1,0:T(8,128)(2,1)} %pad_maximum_fusion.x_ref, bf16[64,2048]{1,0:T(8,128)(2,1)} %copy-done.6, bf16[4,64,512]{2,1,0:T(8,128)(2,1)} %get-tuple-element.11.fold_ref, bf16[4096,512]{1,0:T(8,128)(2,1)} %dout_hbm.1, bf16[672,512]{1,0:T(8,128)(2,1)} %bitcast.71, ...), custom_call_target="tpu_custom_call" | custom-call | tf_op jit(solution)/shard_map/teacher/pallas_call | solution.py:308
  109.5 1.9 %reshape.184.part_ref = bf16[4,16,768]{2,1,0:T(8,128)(2,1)} reshape(bf16[2,512,48]{2,1,0:T(8,128)(2,1)} %teacher.1) | data formatting | bytes 196608 | tf_op jit(solution)/shard_map/reshape | solution.py:473
  111.4 17.5 %token_sum.1 = bf16[4,16,768]{2,1,0:T(8,128)(2,1)} custom-call(bf16[4,16,768]{2,1,0:T(8,128)(2,1)} %reshape.184.part_ref), custom_call_target="tpu_custom_call" | custom-call | tf_op jit(solution)/shard_map/token_sum/pallas_call | solution.py:79
  128.9 1.9 %fusion.4 = f32[1536,96]{0,1:T(8,128)} fusion(bf16[64,768]{1,0:T(8,128)(2,1)} %bitcast.72, s32[]{:T(128)S(6)} %select_n.57, f32[64,1536]{1,0:T(8,128)S(1)} %copy-done.5), kind=kOutput, calls=%fused_computation.27 | convolution fusion | flops 19759104 | bytes 999428 | tf_op jit(solution)/shard_map/dot_general | solution.py:43
  130.8 1.9 %fusion = bf16[64,1536]{1,0:T(8,128)(2,1)S(1)} fusion(bf16[64,768]{1,0:T(8,128)(2,1)} %bitcast.73, bf16[1536,768]{1,0:T(8,128)(2,1)S(1)} %copy-done, f32[64,1536]{1,0:T(8,128)S(1)} %copy-done.5), kind=kOutput, calls=%fused_computation.1 | convolution fusion | flops 152764416 | bytes 3047424 | tf_op jit(solution)/shard_map/dot_general | solution.py:39
  132.7 2.0 %fusion.6 = f32[96,1536]{1,0:T(8,128)} fusion(bf16[64,1536]{1,0:T(8,128)(2,1)S(1)} %fusion, bf16[64,768]{1,0:T(8,128)(2,1)} %copy-done.8, s32[]{:T(128)S(6)} %select_n.57), kind=kOutput, calls=%fused_computation.29 | convolution fusion | flops 18874368 | bytes 802820 | tf_op jit(solution)/shard_map/dot_general | solution.py:43
  134.6 0.8 convolution_convert_fusion.1
  137.2 0.8 copy.48.part_ref
  137.9 8.2 %project_sum.1 = f32[28,16]{1,0:T(8,128)} custom-call(f32[8,28,16]{2,1,0:T(8,128)} %copy.48.part_ref), custom_call_target="tpu_custom_call" | custom-call | tf_op jit(solution)/shard_map/project_sum/pallas_call | solution.py:79
  146.2 1.4 copy.49
  (58 shorter events, 3.1 us)
Async XLA Ops:
  0.6 22.5 %copy-start = (bf16[1536,768]{1,0:T(8,128)(2,1)S(1)}, bf16[1536,768]{1,0:T(8,128)(2,1)}, u32[]{:S(2)}) copy-start(bf16[1536,768]{1,0:T(8,128)(2,1)} %param.14) | copy-start | bytes 7077892
  13.9 5.4 %copy-start.10 = (bf16[4,16,768]{2,1,0:T(8,128)(2,1)S(1)}, bf16[4,16,768]{2,1,0:T(8,128)(2,1)}, u32[]{:S(2)}) copy-start(bf16[4,16,768]{2,1,0:T(8,128)(2,1)} %get-tuple-element.8) | copy-start | bytes 294916
  15.8 0.7 copy-start.6
  19.5 4.9 %copy-start.3 = (f32[4,2,2,2,2,768]{5,4,0,3,2,1:T(2,128)}, f32[4,2,2,2,2,768]{5,4,0,3,2,1:T(2,128)S(1)}, u32[]{:S(2)}) copy-start(f32[4,2,2,2,2,768]{5,4,0,3,2,1:T(2,128)S(1)} %copy.63) | copy-start | bytes 589828
  20.2 4.2 %copy-start.8 = (bf16[64,768]{1,0:T(8,128)(2,1)}, bf16[64,768]{1,0:T(8,128)(2,1)S(1)}, u32[]{:S(2)}) copy-start(bf16[64,768]{1,0:T(8,128)(2,1)S(1)} %multiply_convert_fusion.1) | copy-start | bytes 294916
  22.4 0.8 copy-start.4
  24.3 20.1 %copy-start.11 = (s32[2,32]{1,0:T(2,128)S(1)}, s32[2,32]{1,0:T(2,128)}, u32[]{:S(2)}) copy-start(s32[2,32]{1,0:T(2,128)} %param.11) | copy-start | bytes 772
  49.6 79.3 %copy-start.5 = (f32[64,1536]{1,0:T(8,128)S(1)}, f32[64,1536]{1,0:T(8,128)}, u32[]{:S(2)}) copy-start(f32[64,1536]{1,0:T(8,128)} %copy-done.4) | copy-start | bytes 1179652
  130.8 3.9 %copy-start.1 = (bf16[768,1536]{1,0:T(8,128)(2,1)S(1)}, bf16[768,1536]{1,0:T(8,128)(2,1)}, u32[]{:S(2)}) copy-start(bf16[768,1536]{1,0:T(8,128)(2,1)} %param.13) | copy-start | bytes 7077892
  132.7 2.9 %copy-start.9 = (bf16[4,16,768]{2,1,0:T(8,128)(2,1)S(1)}, bf16[4,16,768]{2,1,0:T(8,128)(2,1)}, u32[]{:S(2)}) copy-start(bf16[4,16,768]{2,1,0:T(8,128)(2,1)} %token_sum.1) | copy-start | bytes 294916
  132.7 2.9 %copy-start.7 = (f32[16,16,48]{2,1,0:T(8,128)S(1)}, f32[16,16,48]{2,1,0:T(8,128)}, u32[]{:S(2)}) copy-start(f32[16,16,48]{2,1,0:T(8,128)} %get-tuple-element.25) | copy-start | bytes 147460
  134.6 2.2 %copy-start.2 = (bf16[2,8,48,224]{3,2,1,0:T(8,128)(2,1)S(1)}, bf16[2,8,48,224]{3,2,1,0:T(8,128)(2,1)}, u32[]{:S(2)}) copy-start(bf16[2,8,48,224]{3,2,1,0:T(8,128)(2,1)} %param.10) | copy-start | bytes 1032196
